TPU v7x, 128 devices: a whole 4x4x4 slice. The times are simulated.
128 devices in a mesh: gy: 8 (over x, z_lo), gz: 16 (over z_hi, y, core).
Axes of the slice: x: 4, y: 4, z: 4 (z_hi: 2, z_lo: 2; z = z_hi * 2 + z_lo), core: 2. Of those that a mesh axis runs over, the one named last changes fastest.
Arguments:
- forcing: bfloat16 [3, 256, 256, 256], P(None, 'gy', 'gz'), may hold values from -10.6 to 10.6
- lift_weight: bfloat16 [20, 3], replicated, may hold values from -3.5 to 3.5
- lift_bias: float32 [20], replicated, may hold values from -3 to 3
- point_weight: bfloat16 [20, 20], replicated, may hold values from -1.25 to 1.25
- spectral_weight: bfloat16 [64, 64, 20, 1280], P('gz', 'gy'), may hold values from -4 to 4
- mixing: float32 [20], replicated, may hold values from 0.3 to 1
- iterate: bfloat16 [20, 256, 256, 256], P(None, 'gy', 'gz'), may hold values from -14.2 to 14.2
- prev_iterate: bfloat16 [20, 256, 256, 256], P(None, 'gy', 'gz'), may hold values from -10.1 to 10.1
- prev_residual: bfloat16 [20, 256, 256, 256], P(None, 'gy', 'gz'), may hold values from -24.1 to 24.1
Outputs:
- next_residual: bfloat16 [20, 256, 256, 256], P(None, 'gy', 'gz')
- mixing_weights: float32 [2], replicated
All inputs are finite; a program needn't handle non-finite values.
Results may differ from a plain program's by a relative error of at most 0.017.
Values may be sent and summed in bfloat16 or wider, within the bound.
A program may use at most 192 MiB of HBM per device.

v0:
```python
import math

import jax
import jax.numpy as jnp
from jax import lax
from jax.sharding import PartitionSpec as P

MODES = 32


REG = 0.001
EPS = 1e-06


def dft_table(length):
    positions = jnp.arange(length, dtype=jnp.int32)[:, None]
    waves = jnp.arange(2 * MODES, dtype=jnp.int32)[None, :]
    wave_number = jnp.where(waves < MODES, waves, waves - MODES + 1)
    angles = (positions * wave_number % length).astype(jnp.float32) * (2.0 * math.pi / length)
    cosine_sine = jnp.where(waves < MODES, jnp.cos(angles), jnp.sin(angles))
    return (cosine_sine.astype(jnp.bfloat16), (cosine_sine * (2.0 / length)).astype(jnp.bfloat16))


def shards(
    forcing,
    lift_weight,
    lift_bias,
    point_weight,
    spectral_weight,
    mixing,
    iterate,
    prev_iterate,
    prev_residual,
):
    channels, rows_y, rows_z, len_x = iterate.shape
    size_y = lax.axis_size("gy")
    size_z = lax.axis_size("gz")
    len_y = rows_y * size_y
    len_z = rows_z * size_z
    modes_all = 2 * MODES
    block_a = modes_all // size_z
    block_k = modes_all // size_y
    ex_fwd, ex_inv = dft_table(len_x)
    ey_fwd, ey_inv = dft_table(len_y)
    ez_fwd, ez_inv = dft_table(len_z)
    ex_fwd_split = ex_fwd.reshape(len_x, size_z, block_a)
    ex_inv_split = ex_inv.reshape(len_x, size_z, block_a)
    ez_fwd_split = ez_fwd.reshape(size_z, rows_z, size_y, block_k)
    ez_inv_split = ez_inv.reshape(size_z, rows_z, size_y, block_k)
    ey_fwd_split = ey_fwd.reshape(size_y, rows_y, modes_all)
    ey_inv_split = ey_inv.reshape(size_y, rows_y, modes_all)
    inject = (
        jnp.einsum("oj,jyzx->oyzx", lift_weight, forcing, preferred_element_type=jnp.float32)
        + lift_bias[:, None, None, None]
    )
    mode_weights = spectral_weight.reshape(
        spectral_weight.shape[0], spectral_weight.shape[1], channels, channels, modes_all
    )

    def z_forward(block):
        return jnp.einsum(
            "sacyz,szgk->gakcy", block, ez_fwd_split, preferred_element_type=jnp.float32
        )

    def x_inverse(block):
        return jnp.einsum(
            "saoyz,xsa->oyzx", block, ex_inv_split, preferred_element_type=jnp.float32
        )

    def forward(state_field):
        along_x = jnp.einsum(
            "cyzx,xsa->sacyz", state_field, ex_fwd_split, preferred_element_type=jnp.float32
        ).astype(jnp.bfloat16)
        moved = lax.all_to_all(along_x, "gz", split_axis=0, concat_axis=0, tiled=True)
        sectioned = z_forward(moved)
        packed = sectioned.astype(jnp.bfloat16)
        turned = lax.all_to_all(packed, "gy", split_axis=0, concat_axis=0, tiled=True)
        return jnp.einsum(
            "gakcy,gyb->akcb", turned, ey_fwd_split, preferred_element_type=jnp.float32
        ).astype(jnp.bfloat16)

    def inverse(mixed_modes):
        spread = jnp.einsum(
            "akob,gyb->gakoy", mixed_modes, ey_inv_split, preferred_element_type=jnp.float32
        ).astype(jnp.bfloat16)
        returned = lax.all_to_all(spread, "gy", split_axis=0, concat_axis=0, tiled=True)
        z_values = jnp.einsum(
            "gakoy,szgk->saoyz", returned, ez_inv_split, preferred_element_type=jnp.float32
        ).astype(jnp.bfloat16)
        at_home = lax.all_to_all(z_values, "gz", split_axis=0, concat_axis=0, tiled=True)
        return x_inverse(at_home)

    def cell(state_field):
        coeffs = forward(state_field)
        mixed_modes = jnp.einsum(
            "akocb,akcb->akob", mode_weights, coeffs, preferred_element_type=jnp.float32
        ).astype(jnp.bfloat16)
        spectral = inverse(mixed_modes)
        pointwise = jnp.einsum(
            "oc,cyzx->oyzx", point_weight, state_field, preferred_element_type=jnp.float32
        )
        return jax.nn.gelu(spectral + pointwise + inject)

    earlier = prev_residual.astype(jnp.float32)
    first_out = cell(iterate)
    current = iterate.astype(jnp.float32)
    newest = first_out - current
    norm_old, cross_term, norm_new = lax.psum(
        (jnp.sum(earlier * earlier), jnp.sum(earlier * newest), jnp.sum(newest * newest)),
        ("gy", "gz"),
    )
    ridge_term = REG * (norm_old + norm_new) + EPS
    denominator = norm_old + norm_new - 2.0 * cross_term + 2.0 * ridge_term
    weight_old = (norm_new + ridge_term - cross_term) / denominator
    weight_new = (norm_old + ridge_term - cross_term) / denominator
    damping = mixing[:, None, None, None]
    next_iterate = (
        weight_old * (prev_iterate.astype(jnp.float32) + damping * earlier)
        + weight_new * (current + damping * newest)
    ).astype(jnp.bfloat16)
    second_out = cell(next_iterate)
    next_residual = (second_out - next_iterate.astype(jnp.float32)).astype(jnp.bfloat16)
    return (next_residual, jnp.stack([weight_old, weight_new]))


def solution(mesh):
    in_specs = (
        P(None, "gy", "gz", None),
        P(),
        P(),
        P(),
        P("gz", "gy", None, None),
        P(),
        P(None, "gy", "gz", None),
        P(None, "gy", "gz", None),
        P(None, "gy", "gz", None),
    )
    out_specs = (P(None, "gy", "gz", None), P())
    return jax.shard_map(shards, mesh=mesh, in_specs=in_specs, out_specs=out_specs, check_vma=False)
```

profile of v0, /device:TPU:1, one launch (start us, length us, event | category | flops | bytes accessed | tf_op | source)
XLA Modules:
  0.0 472.6 jit_solution(14546820031117066645)
XLA Ops:
  0.7 7.3 %fusion.45 = bf16[16,4,20,32,16]{3,0,4,2,1:T(8,128)(2,1)S(1)} fusion(bf16[20,32,16,256]{3,2,1,0:T(8,128)(2,1)} %param.15, s32[16,4]{0,1:T(4,128)S(1)} %add_select_fusion.4, pred[16,4]{0,1:T(4,128)(4,1)S(1)} %fusion.135), kind=kOutput, calls=%fused_computation.60 | convolution fusion | flops 336461824 | bytes 6553920 | tf_op jit(solution)/shard_map/cyzx,xsa->sacyz/dot_general | solution.py:71
  11.7 8.3 %reshape.158 = bf16[16,2,20480]{2,1,0:T(2,128)(2,1)} reshape(bf16[16,4,20,16,32]{4,3,2,1,0:T(8,128)(2,1)} %bitcast.223) | data formatting | bytes 2621440
  20.0 9.6 %all-to-all-start = ((bf16[16,2,20480]{2,1,0:T(2,128)(2,1)}), bf16[16,2,20480]{2,1,0:T(2,128)(2,1)S(1)}, u32[]{:S(2)}, u32[]{:S(2)}) async-start(bf16[16,2,20480]{2,1,0:T(2,128)(2,1)} %reshape.158), calls=%async_computation | async-start | bytes 2621440 | tf_op jit(solution)/shard_map/all_to_all | solution.py:74
  29.6 6.0 %reshape.128 = bf16[4,8,20,20,64]{4,3,1,2,0:T(8,128)(2,1)} reshape(bf16[4,8,20,1280]{3,1,2,0:T(8,128)(2,1)} %param.13) | data formatting | bytes 3276800 | tf_op jit(solution)/shard_map/reshape | solution.py:56
  35.6 14.1 %all-to-all-done = bf16[16,2,20480]{2,1,0:T(2,128)(2,1)S(1)} async-done(((bf16[16,2,20480]{2,1,0:T(2,128)(2,1)}), bf16[16,2,20480]{2,1,0:T(2,128)(2,1)S(1)}, u32[]{:S(2)}, u32[]{:S(2)}) %all-to-all-start) | async-done | bytes 1310752 | tf_op jit(solution)/shard_map/all_to_all | solution.py:74
  53.7 6.1 %fusion.188 = bf16[8,4,20,8,32]{4,3,2,1,0:T(8,128)(2,1)S(1)} fusion(bf16[16,4,20,16,32]{4,3,2,1,0:T(8,128)(2,1)} %reshape.159, s32[8,8]{1,0:T(8,128)S(1)} %add_select_fusion.3, s32[16,16]{1,0:T(8,128)S(1)} %multiply_add_fusion, pred[8,8]{1,0:T(8,128)(4,1)S(1)} %fusion.134), kind=kOutput, calls=%fused_computation.196 | convolution fusion | flops 84312064 | bytes 1639744 | tf_op jit(solution)/shard_map/sacyz,szgk->gakcy/dot_general | solution.py:61
  66.5 6.1 %all-to-all-done.1 = bf16[8,2,10240]{2,1,0:T(2,128)(2,1)S(1)} async-done(((bf16[8,2,10240]{2,1,0:T(2,128)(2,1)}), bf16[8,2,10240]{2,1,0:T(2,128)(2,1)S(1)}, u32[]{:S(2)}, u32[]{:S(2)}) %all-to-all-start.1) | async-done | bytes 327712 | tf_op jit(solution)/shard_map/all_to_all | solution.py:77
  80.8 10.7 %all_to_all.40 = bf16[8,2,10240]{2,1,0:T(2,128)(2,1)S(1)} all-to-all(bf16[8,2,10240]{2,1,0:T(2,128)(2,1)S(1)} %reshape.162), channel_id=1, replica_groups=mesh['gy'=8,'gz'=16] {'gy'}, dimensions={0} | all-to-all | bytes 655360 | tf_op jit(solution)/shard_map/all_to_all | solution.py:86
  97.0 6.8 %fusion.31 = bf16[16,4,20,32,16]{2,4,3,1,0:T(8,128)(2,1)} fusion(bf16[8,4,8,20,32]{3,2,0,4,1:T(8,128)(2,1)S(1)} %copy.29, s32[8,8]{1,0:T(8,128)S(1)} %add_select_fusion.3, s32[16,16]{1,0:T(8,128)S(1)} %multiply_add_fusion, pred[8,8]{1,0:T(8,128)(4,1)S(1)} %fusion.134), kind=kOutput, calls=%fused_computation.46 | convolution fusion | flops 84819968 | bytes 1639744 | tf_op jit(solution)/shard_map/gakoy,szgk->saoyz/dot_general | solution.py:87
  103.8 14.8 %copy.30 = bf16[16,4,20,32,16]{3,4,2,1,0:T(8,128)(2,1)} copy(bf16[16,4,20,32,16]{2,4,3,1,0:T(8,128)(2,1)} %fusion.31) | data formatting | bytes 2621440 | tf_op jit(solution)/shard_map/convert_element_type | solution.py:89
  118.6 8.3 %reshape.164 = bf16[16,2,20480]{2,1,0:T(2,128)(2,1)} reshape(bf16[16,4,20,16,32]{4,3,2,1,0:T(8,128)(2,1)} %bitcast.224) | data formatting | bytes 2621440
  126.9 7.0 %all-to-all-start.3 = ((bf16[16,2,20480]{2,1,0:T(2,128)(2,1)}), bf16[16,2,20480]{2,1,0:T(2,128)(2,1)S(1)}, u32[]{:S(2)}, u32[]{:S(2)}) async-start(bf16[16,2,20480]{2,1,0:T(2,128)(2,1)} %reshape.164), calls=%async_computation.3 | async-start | bytes 2621440 | tf_op jit(solution)/shard_map/all_to_all | solution.py:90
  134.0 5.6 %fusion.93 = f32[20,32,16,256]{3,0,2,1:T(8,128)} fusion(bf16[3,32,16,256]{3,2,1,0:T(8,128)(2,1)S(1)} %copy-done, bf16[20,3]{0,1:T(4,128)(2,1)S(1)} %copy-done.4), kind=kOutput, calls=%fused_computation.84 | convolution fusion | flops 15728640 | bytes 11272312 | tf_op jit(solution)/shard_map/oj,jyzx->oyzx/dot_general | solution.py:53
  139.7 8.7 %fusion.29 = f32[20,32,16,256]{3,0,2,1:T(8,128)} fusion(bf16[20,32,16,256]{3,2,1,0:T(8,128)(2,1)S(1)} %bitcast.222, bf16[20,20]{1,0:T(8,128)(2,1)S(1)} %copy-done.3), kind=kOutput, calls=%fused_computation.44 | convolution fusion | flops 104857600 | bytes 15729440 | tf_op jit(solution)/shard_map/oc,cyzx->oyzx/dot_general | solution.py:99
  148.4 5.7 %all-to-all-done.3 = bf16[16,2,20480]{2,1,0:T(2,128)(2,1)S(1)} async-done(((bf16[16,2,20480]{2,1,0:T(2,128)(2,1)}), bf16[16,2,20480]{2,1,0:T(2,128)(2,1)S(1)}, u32[]{:S(2)}, u32[]{:S(2)}) %all-to-all-start.3) | async-done | bytes 1310752 | tf_op jit(solution)/shard_map/all_to_all | solution.py:90
  158.1 19.0 %copy.31 = bf16[16,4,20,32,16]{0,4,1,3,2:T(8,128)(2,1)} copy(bf16[16,4,20,32,16]{3,4,2,1,0:T(8,128)(2,1)} %bitcast.227) | data formatting | bytes 2621440 | tf_op jit(solution)/shard_map/all_to_all | solution.py:90
  177.1 27.5 %fusion.11 = (f32[]{:T(128)}, f32[]{:T(128)}, f32[]{:T(128)}, f32[20,32,16,256]{3,2,1,0:T(8,128)}) fusion(bf16[20,32,16,256]{3,2,1,0:T(8,128)(2,1)} %param.17, bf16[20,32,16,256]{3,2,1,0:T(8,128)(2,1)} %param.15, f32[20]{0:T(128)S(1)} %copy-done.6, f32[20,32,16,256]{3,0,2,1:T(8,128)} %fusion.93, f32[20,32,16,256]{3,0,2,1:T(8,128)} %fusion.29, ...), kind=kOutput, calls=%fused_computation.20 | convolution fusion | flops 388251648 | bytes 43254172 | tf_op jit(solution)/shard_map/saoyz,xsa->oyzx/dot_general | solution.py:66
  204.5 63.1 %all-reduce = (f32[]{:T(128)}, f32[]{:T(128)}, f32[]{:T(128)}) all-reduce(f32[]{:T(128)} %get-tuple-element.4, f32[]{:T(128)} %get-tuple-element.3, f32[]{:T(128)} %get-tuple-element.2), channel_id=1, replica_groups=mesh['gy'=8,'gz'=16] {'gy','gz'}, use_global_device_ids=true, to_apply=%region_3.4 | all-reduce | flops 3 | bytes 24 | tf_op jit(solution)/shard_map/psum | solution.py:108
  272.2 10.1 %fusion.2 = bf16[20,32,16,256]{3,2,1,0:T(8,128)(2,1)S(1)} fusion(bf16[20,32,16,256]{3,2,1,0:T(8,128)(2,1)} %param.15, bf16[20,32,16,256]{3,2,1,0:T(8,128)(2,1)} %param.17, f32[20,32,16,256]{3,2,1,0:T(8,128)} %get-tuple-element.8, bf16[20,32,16,256]{3,2,1,0:T(8,128)(2,1)} %param.16, f32[]{:T(128)} %div.7, f32[20]{0:T(128)S(1)} %copy-done.5, f32[]{:T(128)} %div.6), kind=kLoop, calls=%fused_computation.11 | loop fusion | flops 28835840 | bytes 31457368 | tf_op jit(solution)/shard_map/convert_element_type | solution.py:120
  291.1 7.5 %reshape.166 = bf16[16,2,20480]{2,1,0:T(2,128)(2,1)S(1)} reshape(bf16[16,4,20,16,32]{4,3,2,1,0:T(8,128)(2,1)} %bitcast.225) | data formatting | bytes 2621440
  298.6 24.3 %all_to_all.41 = bf16[16,2,20480]{2,1,0:T(2,128)(2,1)S(1)} all-to-all(bf16[16,2,20480]{2,1,0:T(2,128)(2,1)S(1)} %reshape.166), channel_id=1, replica_groups=mesh['gy'=8,'gz'=16] {'gz'}, dimensions={0} | all-to-all | bytes 2621440 | tf_op jit(solution)/shard_map/all_to_all | solution.py:74
  327.0 6.1 %fusion.183 = bf16[8,4,20,8,32]{4,3,2,1,0:T(8,128)(2,1)S(1)} fusion(bf16[16,4,20,16,32]{4,3,2,1,0:T(8,128)(2,1)} %reshape.167, s32[8,8]{1,0:T(8,128)S(1)} %add_select_fusion.3, s32[16,16]{1,0:T(8,128)S(1)} %multiply_add_fusion, pred[8,8]{1,0:T(8,128)(4,1)S(1)} %fusion.134), kind=kOutput, calls=%fused_computation.195 | convolution fusion | flops 84312064 | bytes 1639744 | tf_op jit(solution)/shard_map/sacyz,szgk->gakcy/dot_general | solution.py:61
  334.3 9.1 %all_to_all.42 = bf16[8,2,10240]{2,1,0:T(2,128)(2,1)S(1)} all-to-all(bf16[8,2,10240]{2,1,0:T(2,128)(2,1)S(1)} %reshape.168), channel_id=1, replica_groups=mesh['gy'=8,'gz'=16] {'gy'}, dimensions={0} | all-to-all | bytes 655360 | tf_op jit(solution)/shard_map/all_to_all | solution.py:77
  351.6 9.1 %all_to_all.43 = bf16[8,2,10240]{2,1,0:T(2,128)(2,1)S(1)} all-to-all(bf16[8,2,10240]{2,1,0:T(2,128)(2,1)S(1)} %reshape.170), channel_id=1, replica_groups=mesh['gy'=8,'gz'=16] {'gy'}, dimensions={0} | all-to-all | bytes 655360 | tf_op jit(solution)/shard_map/all_to_all | solution.py:86
  366.3 6.8 %fusion.32 = bf16[16,4,20,32,16]{2,4,3,1,0:T(8,128)(2,1)} fusion(bf16[8,4,8,20,32]{3,2,0,4,1:T(8,128)(2,1)S(1)} %copy.42, s32[8,8]{1,0:T(8,128)S(1)} %add_select_fusion.3, s32[16,16]{1,0:T(8,128)S(1)} %multiply_add_fusion, pred[8,8]{1,0:T(8,128)(4,1)S(1)} %fusion.134), kind=kOutput, calls=%fused_computation.47 | convolution fusion | flops 84819968 | bytes 1639744 | tf_op jit(solution)/shard_map/gakoy,szgk->saoyz/dot_general | solution.py:87
  373.0 14.8 %copy.43 = bf16[16,4,20,32,16]{3,4,2,1,0:T(8,128)(2,1)} copy(bf16[16,4,20,32,16]{2,4,3,1,0:T(8,128)(2,1)} %fusion.32) | data formatting | bytes 2621440 | tf_op jit(solution)/shard_map/convert_element_type | solution.py:89
  387.8 8.3 %reshape.172 = bf16[16,2,20480]{2,1,0:T(2,128)(2,1)} reshape(bf16[16,4,20,16,32]{4,3,2,1,0:T(8,128)(2,1)} %bitcast.226) | data formatting | bytes 2621440
  396.2 7.3 %all-to-all-start.7 = ((bf16[16,2,20480]{2,1,0:T(2,128)(2,1)}), bf16[16,2,20480]{2,1,0:T(2,128)(2,1)S(1)}, u32[]{:S(2)}, u32[]{:S(2)}) async-start(bf16[16,2,20480]{2,1,0:T(2,128)(2,1)} %reshape.172), calls=%async_computation.7 | async-start | bytes 2621440 | tf_op jit(solution)/shard_map/all_to_all | solution.py:90
  404.0 10.2 %fusion.27 = f32[32,16,256,20]{2,3,1,0:T(8,128)} fusion(bf16[20,32,16,256]{3,2,1,0:T(8,128)(2,1)} %copy-done.2, bf16[20,20]{1,0:T(8,128)(2,1)S(1)} %copy-done.3), kind=kOutput, calls=%fused_computation.42 | convolution fusion | flops 104857600 | bytes 15729440 | tf_op jit(solution)/shard_map/oc,cyzx->oyzx/dot_general | solution.py:99
  414.3 9.4 %all-to-all-done.7 = bf16[16,2,20480]{2,1,0:T(2,128)(2,1)S(1)} async-done(((bf16[16,2,20480]{2,1,0:T(2,128)(2,1)}), bf16[16,2,20480]{2,1,0:T(2,128)(2,1)S(1)}, u32[]{:S(2)}, u32[]{:S(2)}) %all-to-all-start.7) | async-done | bytes 1310752 | tf_op jit(solution)/shard_map/all_to_all | solution.py:90
  427.7 19.0 %copy.44 = bf16[16,4,20,32,16]{0,4,1,3,2:T(8,128)(2,1)} copy(bf16[16,4,20,32,16]{3,4,2,1,0:T(8,128)(2,1)} %bitcast.228) | data formatting | bytes 2621440 | tf_op jit(solution)/shard_map/all_to_all | solution.py:90
  446.7 25.7 %fusion.22 = bf16[20,32,16,256]{3,2,1,0:T(8,128)(2,1)} fusion(f32[32,16,256,20]{2,3,1,0:T(8,128)} %fusion.27, bf16[20,32,16,256]{3,2,1,0:T(8,128)(2,1)} %copy-done.2, f32[20,32,16,256]{3,0,2,1:T(8,128)} %fusion.93, f32[20]{0:T(128)S(1)} %copy-done.6, bf16[16,4,20,32,16]{0,4,1,3,2:T(8,128)(2,1)} %copy.44, s32[16,4]{0,1:T(4,128)S(1)} %add_select_fusion.4, ...), kind=kOutput, calls=%fused_computation.31 | convolution fusion | flops 372523008 | bytes 32768400 | tf_op jit(solution)/shard_map/saoyz,xsa->oyzx/dot_general | solution.py:66
  (54 shorter events, 64.4 us)
Async XLA Ops:
  0.6 133.4 %copy-start = (bf16[3,32,16,256]{3,2,1,0:T(8,128)(2,1)S(1)}, bf16[3,32,16,256]{3,2,1,0:T(8,128)(2,1)}, u32[]{:S(2)}) copy-start(bf16[3,32,16,256]{3,2,1,0:T(8,128)(2,1)} %param.9) | copy-start | bytes 2359300
  20.0 29.7 %all-to-all-start = ((bf16[16,2,20480]{2,1,0:T(2,128)(2,1)}), bf16[16,2,20480]{2,1,0:T(2,128)(2,1)S(1)}, u32[]{:S(2)}, u32[]{:S(2)}) async-start(bf16[16,2,20480]{2,1,0:T(2,128)(2,1)} %reshape.158), calls=%async_computation | async-start | bytes 2621440 | tf_op jit(solution)/shard_map/all_to_all | solution.py:74
  61.7 10.8 %all-to-all-start.1 = ((bf16[8,2,10240]{2,1,0:T(2,128)(2,1)}), bf16[8,2,10240]{2,1,0:T(2,128)(2,1)S(1)}, u32[]{:S(2)}, u32[]{:S(2)}) async-start(bf16[8,2,10240]{2,1,0:T(2,128)(2,1)} %reshape.160), calls=%async_computation.1 | async-start | bytes 655360 | tf_op jit(solution)/shard_map/all_to_all | solution.py:77
  118.6 15.4 %copy-start.4 = (bf16[20,3]{0,1:T(4,128)(2,1)S(1)}, bf16[20,3]{0,1:T(4,128)(2,1)}, u32[]{:S(2)}) copy-start(bf16[20,3]{0,1:T(4,128)(2,1)} %param.10) | copy-start | bytes 364
  126.9 12.7 %slice-start = ((s8[5242880]{0:T(1024)(128)(4,1)}), s8[1048576]{0:T(1024)(128)(4,1)S(1)}, s32[]{:S(2)}) async-start(s8[5242880]{0:T(1024)(128)(4,1)} %bitcast.221), calls=%async_computation.8 | async-start | bytes 2097152
  126.9 27.1 %all-to-all-start.3 = ((bf16[16,2,20480]{2,1,0:T(2,128)(2,1)}), bf16[16,2,20480]{2,1,0:T(2,128)(2,1)S(1)}, u32[]{:S(2)}, u32[]{:S(2)}) async-start(bf16[16,2,20480]{2,1,0:T(2,128)(2,1)} %reshape.164), calls=%async_computation.3 | async-start | bytes 2621440 | tf_op jit(solution)/shard_map/all_to_all | solution.py:90
  134.0 5.7 %slice-start.1 = ((s8[5242880]{0:T(1024)(128)(4,1)}), s8[4194304]{0:T(1024)(128)(4,1)S(1)}, s32[]{:S(2)}) async-start(s8[5242880]{0:T(1024)(128)(4,1)} %bitcast.221), calls=%async_computation.9 | async-start | bytes 8388608
  134.0 5.7 %copy-start.3 = (bf16[20,20]{1,0:T(8,128)(2,1)S(1)}, bf16[20,20]{1,0:T(8,128)(2,1)}, u32[]{:S(2)}) copy-start(bf16[20,20]{1,0:T(8,128)(2,1)} %param.12) | copy-start | bytes 2404
  158.1 19.0 %copy-start.6 = (f32[20]{0:T(128)S(1)}, f32[20]{0:T(128)}, u32[]{:S(2)}) copy-start(f32[20]{0:T(128)} %param.11) | copy-start | bytes 244
  177.0 95.1 %copy-start.5 = (f32[20]{0:T(128)S(1)}, f32[20]{0:T(128)}, u32[]{:S(2)}) copy-start(f32[20]{0:T(128)} %param.14) | copy-start | bytes 244
  282.3 5.1 %copy-start.2 = (bf16[20,32,16,256]{3,2,1,0:T(8,128)(2,1)}, bf16[20,32,16,256]{3,2,1,0:T(8,128)(2,1)S(1)}, u32[]{:S(2)}) copy-start(bf16[20,32,16,256]{3,2,1,0:T(8,128)(2,1)S(1)} %fusion.2) | copy-start | bytes 15728644
  396.2 27.4 %all-to-all-start.7 = ((bf16[16,2,20480]{2,1,0:T(2,128)(2,1)}), bf16[16,2,20480]{2,1,0:T(2,128)(2,1)S(1)}, u32[]{:S(2)}, u32[]{:S(2)}) async-start(bf16[16,2,20480]{2,1,0:T(2,128)(2,1)} %reshape.172), calls=%async_computation.7 | async-start | bytes 2621440 | tf_op jit(solution)/shard_map/all_to_all | solution.py:90
  446.7 25.7 %copy-start.1 = (bf16[3,32,16,256]{3,2,1,0:T(8,128)(2,1)S(1)}, bf16[3,32,16,256]{3,2,1,0:T(8,128)(2,1)}, u32[]{:S(2)}) copy-start(bf16[3,32,16,256]{3,2,1,0:T(8,128)(2,1)} %param.9) | copy-start | bytes 2359300
where the time goes:
time: 480 us; the launch traced here: 473 us
  local copies, waits for them, and re-layouts  148 us (31%)
  matrix products  120 us (25%)
  blocking collectives  116 us (24%)
  waiting for transfers between devices  35.2 us (7%)
  starting transfers between devices  28.6 us (6%)
  other arithmetic  18.6 us (4%)
  between operations  5.69 us (1%)
    psum x1, blocking collectives, shards(): lax.psum((jnp.sum(earlier * earlier), jnp.sum(earlier * newest), jnp.sum(...  63.1 us
    unnamed x34, local copies, waits for them, and re-layouts  58.8 us
    dot_general x2, matrix products, x_inverse(): jnp.einsum('saoyz,xsa->oyzx', block, ex_inv_split, preferred_element_type...  53.2 us
    all_to_all x2, local copies, waits for them, and re-layouts, inverse(): lax.all_to_all(z_values, 'gz', split_axis=0, concat_axis=0, tiled=True)  38 us
    convert_element_type x2, local copies, waits for them, and re-layouts, inverse(): z_values = jnp.einsum('gakoy,szgk->saoyz', returned, ez_inv_split, prefer...  29.6 us
    all_to_all x1, blocking collectives, forward(): lax.all_to_all(along_x, 'gz', split_axis=0, concat_axis=0, tiled=True)  24.3 us
    all_to_all x2, blocking collectives, inverse(): lax.all_to_all(spread, 'gy', split_axis=0, concat_axis=0, tiled=True)  19.9 us
    dot_general x2, matrix products, cell(): jnp.einsum('oc,cyzx->oyzx', point_weight, state_field, preferred_element_...  18.9 us
  transfers between devices with their start and end apart: 4, of which 4 were waited for; matrix products, arithmetic and copies ran while one was open for 7% of the time, Pallas kernels for 0%

commit v1 on v0

v1 whole, which is shorter than its diff:
```python
import functools
import math

import jax
import jax.numpy as jnp
import ml_dtypes
import numpy as np
from jax import lax
from jax.experimental import pallas as pl
from jax.experimental.pallas import tpu as pltpu
from jax.sharding import PartitionSpec as P

MESH = pl.DeviceIdType.MESH
BF = jnp.bfloat16
F32 = jnp.float32

MODES = 32
KM = 64
REG = 0.001
EPS = 1e-06

C = 20
LEN = 256
NGY = 8
NQ = 8
NH = 2
RY = 32
RZ = 16
GROUPS = 4
GY = 8
BA = 4
BK = 8
ROWS = C * NH * BA
HALF = C * BA


def dft_table(length):
    positions = np.arange(length)[:, None]
    waves = np.arange(2 * MODES)[None, :]
    number = np.where(waves < MODES, waves, waves - MODES + 1)
    angles = (positions * number % length).astype(np.float32) * np.float32(2.0 * math.pi / length)
    both = np.where(waves < MODES, np.cos(angles), np.sin(angles)).astype(np.float32)
    inverse = (both * np.float32(2.0 / length)).astype(ml_dtypes.bfloat16)
    return both.astype(ml_dtypes.bfloat16), inverse


@functools.lru_cache(maxsize=None)
def tables():
    fwd, inv = dft_table(LEN)
    f = fwd.astype(np.float32)
    i = inv.astype(np.float32)
    order = np.arange(KM).reshape(NH, NQ, BA).transpose(1, 0, 2).reshape(-1)
    ex = f[:, order].T
    ix = i[:, order].T
    eye_y = np.eye(GY, dtype=np.float32)
    eye_k = np.eye(BK, dtype=np.float32)
    kz = np.einsum("hqzgk,yw->hqyzgwk", f.reshape(NH, NQ, RZ, NGY, BK), eye_y)
    kz = kz.reshape(NH, NQ * GY * RZ, NGY * GY * BK)
    kzi = np.einsum("hqzgk,yw->hgykqwz", i.reshape(NH, NQ, RZ, NGY, BK), eye_y)
    kzi = kzi.reshape(NH, NGY * GY * BK, NQ * GY * RZ)
    ky = np.einsum("yb,kj->ykjb", f, eye_k).reshape(LEN * BK, BK * KM)
    kyi = np.einsum("yb,kj->kbyj", i, eye_k).reshape(BK * KM, LEN * BK)
    return tuple(np.ascontiguousarray(t).astype(ml_dtypes.bfloat16) for t in (ex, ix, kz, kzi, ky, kyi))


def iota(shape, axis):
    return lax.broadcasted_iota(jnp.int32, shape, axis)


def dot(a, b):
    return jnp.dot(a, b, preferred_element_type=F32)


def dot_nt(a, b):
    return lax.dot_general(a, b, (((1,), (1,)), ((), ())), preferred_element_type=F32)


def swap_rows(first, second):
    low = iota(first.shape, 1) < BA
    return (
        jnp.where(low, first, pltpu.roll(second, BA, 1)),
        jnp.where(low, pltpu.roll(first, BA, 1), second),
    )


def swap_lanes(first, second):
    axis = first.ndim - 1
    low = iota(first.shape, axis) < 64
    return (
        jnp.where(low, first, pltpu.roll(second, 64, axis)),
        jnp.where(low, pltpu.roll(first, 64, axis), second),
    )


def gelu(x):
    inner = x * (math.sqrt(2.0 / math.pi) + (math.sqrt(2.0 / math.pi) * 0.044715) * (x * x))
    half = 0.5 * x
    return half + half * jnp.tanh(inner)


def kernel(
    forcing, lift_w, lift_b, point_w, spec_w, mixing, iterate, prev_it, prev_res,
    ex, ix, kz_all, kzi_all, ky_hbm, kyi_hbm,
    out, weights_out,
    v, pit, pres, step, forc, wts, lhs, xs, xr, bs, br, pf, ps, pr, gs, gr, hs, hg,
    kz, kzi, ky, kyi, qm, mo, osc, acc, ar1, ar2, ones,
    load_sem, in_sem, out_sem, loc_sem,
    xs_sem, xr_sem, bs_sem, br_sem, ps_sem, pr_sem, gs_sem, gr_sem, hs_sem, hr_sem, zs_sem, zr_sem,
    s1_sem, r1_sem, s2_sem, r2_sem,
):
    gy = lax.axis_index("gy")
    gz = lax.axis_index("gz")
    h = gz // NQ
    q = gz % NQ

    barrier = pltpu.get_barrier_semaphore()
    for off in range(1, 16):
        pl.semaphore_signal(barrier, inc=1, device_id=(gy, (gz + off) % 16), device_id_type=MESH)
    for off in range(1, NGY):
        pl.semaphore_signal(barrier, inc=1, device_id=((gy + off) % NGY, gz), device_id_type=MESH)

    in_copies = [
        pltpu.make_async_copy(
            iterate.at[:, pl.ds(g * GY, GY)], v.at[:, pl.ds(g * GY, GY)], in_sem.at[g]
        )
        for g in range(GROUPS)
    ]
    loads = {
        name: pltpu.make_async_copy(src, dst, load_sem.at[n])
        for n, (name, src, dst) in enumerate([
            ("kz", kz_all.at[h], kz),
            ("ky", ky_hbm, ky),
            ("wts", spec_w, wts),
            ("kyi", kyi_hbm, kyi),
            ("kzi", kzi_all.at[h], kzi),
            ("forc", forcing, forc),
            ("pres", prev_res, pres),
            ("pit", prev_it, pit),
        ])
    }
    for copy in in_copies:
        copy.start()
    for copy in loads.values():
        copy.start()

    def send_x(g, off):
        dest = (q + off) % NQ
        return pltpu.make_async_remote_copy(
            xs.at[g, dest], xr.at[g, q], xs_sem.at[g, off], xr_sem.at[g, off],
            device_id=(gy, h * NQ + dest), device_id_type=MESH)

    def send_b(g, off):
        dest = (q + off) % NQ
        return pltpu.make_async_remote_copy(
            bs.at[g, dest], br.at[g, q], bs_sem.at[g, off], br_sem.at[g, off],
            device_id=(gy, h * NQ + dest), device_id_type=MESH)

    partner = (gy, (1 - h) * NQ + q)

    def send_p(g):
        return pltpu.make_async_remote_copy(
            ps.at[g, 1 - h], pr.at[g], ps_sem.at[g], pr_sem.at[g],
            device_id=partner, device_id_type=MESH)

    def send_z(p):
        return pltpu.make_async_remote_copy(
            hg.at[p, h], hg.at[p, h], zs_sem.at[p], zr_sem.at[p],
            device_id=partner, device_id_type=MESH)

    def recv_z(p):
        return pltpu.make_async_remote_copy(
            hg.at[p, h], hg.at[p, 1 - h], zs_sem.at[p], zr_sem.at[p],
            device_id=partner, device_id_type=MESH)

    def send_g(p, off):
        dest = (gy + off) % NGY
        return pltpu.make_async_remote_copy(
            gs.at[p, dest], gr.at[p, gy], gs_sem.at[p, off], gr_sem.at[p, off],
            device_id=(dest, gz), device_id_type=MESH)

    def send_h(p, off):
        dest = (gy + off) % NGY
        return pltpu.make_async_remote_copy(
            hs.at[p, dest], hg.at[p, h, gy], hs_sem.at[p, off], hr_sem.at[p, off],
            device_id=(dest, gz), device_id_type=MESH)

    def own_x(g):
        return pltpu.make_async_copy(xs.at[g, q], xr.at[g, q], loc_sem.at[g])

    def own_b(g):
        return pltpu.make_async_copy(bs.at[g, q], br.at[g, q], loc_sem.at[4 + g])

    def own_g(p):
        return pltpu.make_async_copy(gs.at[p, gy], gr.at[p, gy], loc_sem.at[8 + p])

    def own_h(p):
        return pltpu.make_async_copy(hs.at[p, gy], hg.at[p, h, gy], loc_sem.at[10 + p])

    def x_stage(g):
        for pair in range(C // 2):
            parts = []
            for j in range(2):
                field = v[2 * pair + j, pl.ds(g * GY, GY)].reshape(GY * RZ, LEN)
                parts.append(dot_nt(ex[...], field).reshape(NQ, NH * BA, GY * RZ))
            xs[g, :, pair * 16:(pair + 1) * 16, :] = jnp.concatenate(parts, axis=1).astype(BF)

    def z_stage(g):
        left = jnp.concatenate([xr[g, s] for s in range(NQ)], axis=1)
        part = dot(left, kz[...]).reshape(C // 2, 2, 8, 512)
        zero, one = swap_rows(part[:, 0], part[:, 1])
        zero = zero.reshape(HALF, 512)
        one = one.reshape(HALF, 512)
        pf[g, 0] = zero
        pf[g, 1] = one
        ps[g, 0] = zero.astype(BF)
        ps[g, 1] = one.astype(BF)

    def join_stage(p):
        first = pf[2 * p, h] + pr[2 * p].astype(F32)
        second = pf[2 * p + 1, h] + pr[2 * p + 1].astype(F32)
        for j in range(4):
            cut = slice(j * 128, (j + 1) * 128)
            even, odd = swap_lanes(first[:, cut], second[:, cut])
            gs[p, 2 * j] = even.astype(BF)
            gs[p, 2 * j + 1] = odd.astype(BF)

    def y_stage():
        left = jnp.concatenate([gr[p, s] for s in range(NGY) for p in range(2)], axis=1)
        modes = dot(left, ky[...]).astype(BF).astype(F32).reshape(C // 2, 8, 512)
        for m in range(4):
            here = modes[:, :, m * 128:(m + 1) * 128]
            there = pltpu.roll(here, BA, 1)
            even, odd = swap_lanes(here, there)
            qm[2 * m] = even
            qm[2 * m + 1] = odd

    def mix_stage():
        def one_pair(m, carry):
            for a in range(BA):
                sums = []
                for j in range(2):
                    k = 2 * m + j
                    total = jnp.zeros((C, 128), F32)
                    for t in range(C // 2):
                        w = wts[a, k, :, t * 128:(t + 1) * 128].astype(F32)
                        total = total + w * qm[k, t, a:a + 1, :]
                    sums.append(total + pltpu.roll(total, 64, 1))
                low = iota((C, 128), 1) < 64
                mo[m, pl.ds(a, C, stride=BA), :] = jnp.where(low, sums[0], sums[1])
            return carry

        lax.fori_loop(0, 4, one_pair, 0)

    def yi_stage():
        left = jnp.concatenate([mo[m].astype(BF) for m in range(4)], axis=1)
        for s in range(NGY):
            back = dot(left, kyi[:, s * 256:(s + 1) * 256]).astype(BF)
            hs[0, s] = back[:, :128]
            hs[1, s] = back[:, 128:]

    def zi_stage(p):
        cuts = {}
        for half in range(NH):
            for j in range(4):
                one = hg[p, half, 2 * j].astype(F32)
                two = hg[p, half, 2 * j + 1].astype(F32)
                cuts[half, j] = swap_lanes(one, two)
        for e in range(2):
            zero = jnp.concatenate([cuts[0, j][e] for j in range(4)], axis=1).reshape(C // 2, 8, 512)
            one = jnp.concatenate([cuts[1, j][e] for j in range(4)], axis=1).reshape(C // 2, 8, 512)
            even, odd = swap_rows(zero, one)
            left = jnp.concatenate([even, odd], axis=1).reshape(ROWS, 512).astype(BF)
            for s in range(0, NQ, 2):
                back = dot(left, kzi[:, s * 128:(s + 2) * 128]).astype(BF)
                bs[2 * p + e, s] = back[:, :128]
                bs[2 * p + e, s + 1] = back[:, 128:]

    def build_lhs():
        rows_o = iota((C * RZ, C), 0) // RZ
        pick = jnp.where(rows_o == iota((C * RZ, C), 1), 1.0, 0.0).astype(BF)
        col = iota((C, C * RZ), 1) // RZ
        spread = jnp.where(col == iota((C, C * RZ), 0), 1.0, 0.0).astype(BF)
        wide = dot(dot(pick, point_w[...]).astype(BF), spread)
        same = iota((C * RZ, C * RZ), 0) % RZ == iota((C * RZ, C * RZ), 1) % RZ
        wide = jnp.where(same, wide, 0.0)
        col3 = iota((3, 3 * RZ), 1) // RZ
        spread3 = jnp.where(col3 == iota((3, 3 * RZ), 0), 1.0, 0.0).astype(BF)
        lift = dot(dot(pick, lift_w[...]).astype(BF), spread3)
        same3 = iota((C * RZ, 3 * RZ), 0) % RZ == iota((C * RZ, 3 * RZ), 1) % RZ
        lift = jnp.where(same3, lift, 0.0)
        bias = lift_b[...]
        hi = bias.astype(BF).astype(F32)
        mid = (bias - hi).astype(BF).astype(F32)
        lo = (bias - hi - mid).astype(BF).astype(F32)
        row = iota((16, C), 0)
        pieces = jnp.where(row == 0, hi, jnp.where(row == 1, mid, jnp.where(row == 2, lo, 0.0)))
        bias_cols = dot_nt(pick, pieces.astype(BF))
        full = jnp.concatenate([wide, lift, bias_cols], axis=1).astype(BF)
        for y in range(GY):
            lhs[y, :, 0:384] = full
        ones[...] = jnp.ones((16, LEN), BF)

    def turn_stage(g):
        for pair in range(C // 2):
            tile = br[g, :, pair * 16:(pair + 1) * 16, :].astype(F32)
            for j in range(2):
                block = tile[:, 8 * j:8 * j + 8].reshape(KM, GY * RZ)
                turned = jnp.transpose(block, (1, 0)).astype(BF).reshape(GY, RZ, KM)
                o = 2 * pair + j
                lhs[:, o * RZ:(o + 1) * RZ, 384:448] = turned

    def field_row(y):
        return v[:, y].reshape(C * RZ, LEN)

    def pre_activation(yl, y):
        right = jnp.concatenate(
            [field_row(y), forc[:, y].reshape(3 * RZ, LEN), ones[...], ix[...]], axis=0)
        osc[...] = dot(lhs[yl][:, :448], right)

    def final_first(g):
        turn_stage(g)

        def row(yl, carry):
            y = g * GY + yl
            pre_activation(yl, y)
            s_oo = jnp.zeros((RZ, LEN), F32)
            s_on = jnp.zeros((RZ, LEN), F32)
            s_nn = jnp.zeros((RZ, LEN), F32)
            for o in range(C):
                current = v[o, y].astype(F32)
                earlier = pres[o, y].astype(F32)
                newest = gelu(osc[o * RZ:(o + 1) * RZ, :]) - current
                step[o, y] = current + mixing[o] * newest
                s_oo += earlier * earlier
                s_on += earlier * newest
                s_nn += newest * newest
            acc[0] += s_oo
            acc[1] += s_on
            acc[2] += s_nn
            return carry

        lax.fori_loop(0, GY, row, 0)

    def final_second(g):
        turn_stage(g)

        def row(yl, carry):
            y = g * GY + yl
            pre_activation(yl, y)
            for o in range(C):
                current = v[o, y].astype(F32)
                pres[o, y] = (gelu(osc[o * RZ:(o + 1) * RZ, :]) - current).astype(BF)
            return carry

        lax.fori_loop(0, GY, row, 0)

    def combine(g, w_old, w_new):
        def one(c, carry):
            ys = pl.ds(g * GY, GY)
            old = pit[c, ys].astype(F32) + mixing[c] * pres[c, ys].astype(F32)
            v[c, ys] = (w_old * old + w_new * step[c, ys]).astype(BF)
            return carry

        lax.fori_loop(0, C, one, 0)

    def cell(number, w_old=None, w_new=None):
        first = number == 0
        for g in range(GROUPS):
            if first:
                in_copies[g].wait()
            else:
                combine(g, w_old, w_new)
            x_stage(g)
            if first and g == 0:
                pl.semaphore_wait(barrier, 22)
            for off in range(1, NQ):
                send_x(g, off).start()
            own_x(g).start()
        if first:
            acc[...] = jnp.zeros((3, RZ, LEN), F32)
            build_lhs()
            loads["kz"].wait()

        def z_part(g):
            own_x(g).wait()
            for off in range(1, NQ):
                send_x(g, off).wait_recv()
            z_stage(g)
            send_p(g).start()

        def join_part(p):
            send_p(2 * p).wait_recv()
            send_p(2 * p + 1).wait_recv()
            join_stage(p)
            for off in range(1, NGY):
                send_g(p, off).start()
            own_g(p).start()

        z_part(0)
        z_part(1)
        z_part(2)
        join_part(0)
        z_part(3)
        join_part(1)
        if first:
            for name in ("ky", "wts", "kyi", "kzi", "forc", "pres"):
                loads[name].wait()
        for p in range(2):
            own_g(p).wait()
            for off in range(1, NGY):
                send_g(p, off).wait_recv()
        y_stage()
        mix_stage()
        yi_stage()
        for p in range(2):
            for off in range(1, NGY):
                send_h(p, off).start()
            own_h(p).start()
        for p in range(2):
            own_h(p).wait()
            for off in range(1, NGY):
                send_h(p, off).wait_recv()
            send_z(p).start()
        for p in range(2):
            recv_z(p).wait_recv()
            zi_stage(p)
            for g in (2 * p, 2 * p + 1):
                for off in range(1, NQ):
                    send_b(g, off).start()
                own_b(g).start()
        for g in range(GROUPS):
            own_b(g).wait()
            for off in range(1, NQ):
                send_b(g, off).wait_recv()
            if first:
                final_first(g)
            else:
                final_second(g)
                ys = pl.ds(g * GY, GY)
                pltpu.make_async_copy(pres.at[:, ys], out.at[:, ys], out_sem.at[g]).start()
        for g in range(GROUPS):
            for off in range(1, NQ):
                send_x(g, off).wait_send()
                send_b(g, off).wait_send()
            send_p(g).wait_send()
        for p in range(2):
            send_z(p).wait_send()
            for off in range(1, NGY):
                send_g(p, off).wait_send()
                send_h(p, off).wait_send()

    def reduce_norms():
        rows = iota((8, 128), 0)
        mine = jnp.zeros((8, 128), F32)
        for n in range(3):
            total = jnp.sum(acc[n], axis=0, keepdims=True)
            mine = jnp.where(rows == n, total[:, :128] + total[:, 128:], mine)
        ar1[gz] = mine
        sends = [
            pltpu.make_async_remote_copy(
                ar1.at[gz], ar1.at[gz], s1_sem.at[off], r1_sem.at[off],
                device_id=(gy, (gz + off) % 16), device_id_type=MESH)
            for off in range(1, 16)
        ]
        for copy in sends:
            copy.start()
        for off in range(1, 16):
            src = (gz - off + 16) % 16
            pltpu.make_async_remote_copy(
                ar1.at[gz], ar1.at[src], s1_sem.at[off], r1_sem.at[off],
                device_id=(gy, src), device_id_type=MESH).wait_recv()
        total = ar1[0]
        for s in range(1, 16):
            total = total + ar1[s]
        ar2[gy] = total
        sends2 = [
            pltpu.make_async_remote_copy(
                ar2.at[gy], ar2.at[gy], s2_sem.at[off], r2_sem.at[off],
                device_id=((gy + off) % NGY, gz), device_id_type=MESH)
            for off in range(1, NGY)
        ]
        for copy in sends2:
            copy.start()
        for off in range(1, NGY):
            src = (gy - off + NGY) % NGY
            pltpu.make_async_remote_copy(
                ar2.at[gy], ar2.at[src], s2_sem.at[off], r2_sem.at[off],
                device_id=(src, gz), device_id_type=MESH).wait_recv()
        total = ar2[0]
        for s in range(1, NGY):
            total = total + ar2[s]
        for copy in sends + sends2:
            copy.wait_send()
        sums = jnp.sum(total, axis=1, keepdims=True)
        norm_old, cross, norm_new = sums[0:1], sums[1:2], sums[2:3]
        ridge = REG * (norm_old + norm_new) + EPS
        denominator = norm_old + norm_new - 2.0 * cross + 2.0 * ridge
        w_old = (norm_new + ridge - cross) / denominator
        w_new = (norm_old + ridge - cross) / denominator
        lane = iota((8, 128), 1)
        weights_out[...] = jnp.where(lane == 0, w_old, w_new)
        return w_old.reshape(1, 1, 1), w_new.reshape(1, 1, 1)

    cell(0)
    w_old, w_new = reduce_norms()
    loads["pit"].wait()
    cell(1, w_old, w_new)
    for g in range(GROUPS):
        ys = pl.ds(g * GY, GY)
        pltpu.make_async_copy(pres.at[:, ys], out.at[:, ys], out_sem.at[g]).wait()


def shards(forcing, lift_weight, lift_bias, point_weight, spectral_weight, mixing, iterate, prev_iterate, prev_residual):
    ex, ix, kz, kzi, ky, kyi = (jnp.asarray(t) for t in tables())
    field = (C, RY, RZ, LEN)
    vmem = pl.BlockSpec(memory_space=pltpu.VMEM)
    smem = pl.BlockSpec(memory_space=pltpu.SMEM)
    hbm = pl.BlockSpec(memory_space=pl.ANY)
    dma = pltpu.SemaphoreType.DMA
    scratch = [
        pltpu.VMEM(field, BF),
        pltpu.VMEM(field, BF),
        pltpu.VMEM(field, BF),
        pltpu.VMEM(field, F32),
        pltpu.VMEM((3, RY, RZ, LEN), BF),
        pltpu.VMEM((BA, BK, C, C * KM), BF),
        pltpu.VMEM((GY, C * RZ, 512), BF),
        pltpu.VMEM((GROUPS, NQ, ROWS, 128), BF),
        pltpu.VMEM((GROUPS, NQ, ROWS, 128), BF),
        pltpu.VMEM((GROUPS, NQ, ROWS, 128), BF),
        pltpu.VMEM((GROUPS, NQ, ROWS, 128), BF),
        pltpu.VMEM((GROUPS, NH, HALF, 512), F32),
        pltpu.VMEM((GROUPS, NH, HALF, 512), BF),
        pltpu.VMEM((GROUPS, HALF, 512), BF),
        pltpu.VMEM((2, NGY, HALF, 128), BF),
        pltpu.VMEM((2, NGY, HALF, 128), BF),
        pltpu.VMEM((2, NGY, HALF, 128), BF),
        pltpu.VMEM((2, NH, NGY, HALF, 128), BF),
        pltpu.VMEM((1024, 512), BF),
        pltpu.VMEM((512, 1024), BF),
        pltpu.VMEM((2048, 512), BF),
        pltpu.VMEM((512, 2048), BF),
        pltpu.VMEM((BK, C // 2, 8, 128), F32),
        pltpu.VMEM((4, HALF, 128), F32),
        pltpu.VMEM((C * RZ, LEN), F32),
        pltpu.VMEM((3, RZ, LEN), F32),
        pltpu.VMEM((16, 8, 128), F32),
        pltpu.VMEM((NGY, 8, 128), F32),
        pltpu.VMEM((16, LEN), BF),
        dma((8,)), dma((GROUPS,)), dma((GROUPS,)), dma((12,)),
        dma((GROUPS, NQ)), dma((GROUPS, NQ)), dma((GROUPS, NQ)), dma((GROUPS, NQ)),
        dma((GROUPS,)), dma((GROUPS,)),
        dma((2, NGY)), dma((2, NGY)), dma((2, NGY)), dma((2, NGY)),
        dma((2,)), dma((2,)),
        dma((16,)), dma((16,)), dma((NGY,)), dma((NGY,)),
    ]
    result, weights = pl.pallas_call(
        kernel,
        out_shape=(
            jax.ShapeDtypeStruct(field, BF),
            jax.ShapeDtypeStruct((8, 128), F32),
        ),
        in_specs=[hbm, vmem, vmem, vmem, hbm, smem, hbm, hbm, hbm, vmem, vmem, hbm, hbm, hbm, hbm],
        out_specs=(hbm, vmem),
        scratch_shapes=scratch,
        compiler_params=pltpu.CompilerParams(
            collective_id=0, has_side_effects=True, vmem_limit_bytes=60 * 1024 * 1024),
        cost_estimate=pl.CostEstimate(
            flops=10_000_000_000, bytes_accessed=40_000_000, transcendentals=5_000_000),
    )(forcing, lift_weight, lift_bias.reshape(1, C), point_weight, spectral_weight, mixing,
      iterate, prev_iterate, prev_residual, ex, ix, kz, kzi, ky, kyi)
    return result, weights[0, :2]


def solution(mesh):
    in_specs = (
        P(None, "gy", "gz", None),
        P(),
        P(),
        P(),
        P("gz", "gy", None, None),
        P(),
        P(None, "gy", "gz", None),
        P(None, "gy", "gz", None),
        P(None, "gy", "gz", None),
    )
    out_specs = (P(None, "gy", "gz", None), P())
    return jax.shard_map(shards, mesh=mesh, in_specs=in_specs, out_specs=out_specs, check_vma=False)
```

time: 480 us -> 155 us (0.32); the launches traced: 473 us -> 155 us
  Pallas kernels: 0 us -> 143 us
  local copies, waits for them, and re-layouts: 148 us -> 10.9 us
  matrix products: 120 us -> 0 us
  blocking collectives: 116 us -> 0 us
  waiting for transfers between devices: 35.2 us -> 0 us
  starting transfers between devices: 28.6 us -> 0 us
  other arithmetic: 18.6 us -> 0 us
  between operations: 5.69 us -> 0.64 us
    pallas_call x0 -> x1, Pallas kernels: none -> 143 us  [shards(): pl.pallas_call(kernel, out_shape=(jax.ShapeDtypeStruct(field, BF), jax.Sh...]
    dot_general x15 -> x0, matrix products: 120 us -> none  [the longest x2 53.2 us: x_inverse(): jnp.einsum('saoyz,xsa->oyzx', block, ex_inv_split, preferred_element_type...]
    psum x1 -> x0, blocking collectives: 63.1 us -> none  [shards(): lax.psum((jnp.sum(earlier * earlier), jnp.sum(earlier * newest), jnp.sum(...]
    all_to_all x4 -> x0, blocking collectives: 53.3 us -> none  [the longest x1 24.3 us: forward(): lax.all_to_all(along_x, 'gz', split_axis=0, concat_axis=0, tiled=True)]
    unnamed x34 -> x3, local copies, waits for them, and re-layouts: 58.8 us -> 9.7 us
    all_to_all x4 -> x0, local copies, waits for them, and re-layouts: 45.5 us -> none  [the longest x2 38 us: inverse(): lax.all_to_all(z_values, 'gz', split_axis=0, concat_axis=0, tiled=True)]
    convert_element_type x6 -> x0, local copies, waits for them, and re-layouts: 37.4 us -> none  [the longest x2 29.6 us: inverse(): z_values = jnp.einsum('gakoy,szgk->saoyz', returned, ez_inv_split, prefer...]
    all_to_all x4 -> x0, waiting for transfers between devices: 35.2 us -> none  [the longest x2 15.1 us: inverse(): lax.all_to_all(z_values, 'gz', split_axis=0, concat_axis=0, tiled=True)]
  transfers between devices with their start and end apart: 4 -> 0, of which waited for: 4 -> 0; matrix products, arithmetic and copies ran while one was open for 7% -> 0% of each run, Pallas kernels for 0% -> 0%
where the time goes in v1:
time: 155 us
  Pallas kernels  143 us (92%)
  local copies, waits for them, and re-layouts  10.9 us (7%)
    pallas_call x1, Pallas kernels, shards(): pl.pallas_call(kernel, out_shape=(jax.ShapeDtypeStruct(field, BF), jax.Sh...  143 us
    unnamed x3, local copies, waits for them, and re-layouts  9.7 us

profile of v1, /device:TPU:1, one launch (start us, length us, event | category | flops | bytes accessed | tf_op | source)
XLA Modules:
  0.0 154.6 jit_solution(163635127374186061)
XLA Ops:
  0.6 1.4 copy.17.lift_w
  2.0 3.0 %copy.18.spec_w = bf16[4,8,20,1280]{3,2,1,0:T(8,128)(2,1)} copy(bf16[4,8,20,1280]{3,1,2,0:T(8,128)(2,1)} %param.19) | data formatting | bytes 3276800 | tf_op args[4]
  5.0 143.1 %shard_map.158 = (bf16[20,32,16,256]{3,2,1,0:T(8,128)(2,1)}, f32[8,128]{1,0:T(8,128)}) custom-call(bf16[3,32,16,256]{3,2,1,0:T(8,128)(2,1)} %forcing.1, bf16[20,3]{1,0:T(8,128)(2,1)} %copy.17.lift_w, f32[1,20]{1,0:T(1,128)} %bitcast.3, bf16[20,20]{1,0:T(8,128)(2,1)} %point_w.1, bf16[4,8,20,1280]{3,2,1,0:T(8,128)(2,1)} %copy.18.spec_w, f32[20]{0:T(128)} %mixing.1, ...), custom_call_target="tpu_custom_call" | custom-call | flops 10000000000 | bytes 40000000 | tf_op jit(solution)/shard_map/pallas_call | solution.py:557
  148.1 1.2 slice_bitcast_fusion
  149.3 5.3 %copy.20 = bf16[20,32,16,256]{3,2,1,0:T(8,128)(2,1)} copy(bf16[20,32,16,256]{3,2,1,0:T(8,128)(2,1)} %get-tuple-element.8) | data formatting | bytes 10485760

commit v2 on v1

v2 whole, which is shorter than its diff:
```python
import functools
import math

import jax
import jax.numpy as jnp
import ml_dtypes
import numpy as np
from jax import lax
from jax.experimental import pallas as pl
from jax.experimental.pallas import tpu as pltpu
from jax.sharding import PartitionSpec as P

MESH = pl.DeviceIdType.MESH
BF = jnp.bfloat16
F32 = jnp.float32

MODES = 32
KM = 64
REG = 0.001
EPS = 1e-06

C = 20
LEN = 256
NGY = 8
NQ = 8
NH = 2
RY = 32
RZ = 16
GROUPS = 4
GY = 8
BA = 4
BK = 8
ROWS = C * NH * BA
HALF = C * BA


PEERS = [(dh, off) for off in range(NGY) for dh in range(NH) if (dh, off) != (0, 0)]


def dft_table(length):
    positions = np.arange(length)[:, None]
    waves = np.arange(2 * MODES)[None, :]
    number = np.where(waves < MODES, waves, waves - MODES + 1)
    angles = (positions * number % length).astype(np.float32) * np.float32(2.0 * math.pi / length)
    both = np.where(waves < MODES, np.cos(angles), np.sin(angles)).astype(np.float32)
    inverse = (both * np.float32(2.0 / length)).astype(ml_dtypes.bfloat16)
    return both.astype(ml_dtypes.bfloat16), inverse


@functools.lru_cache(maxsize=None)
def tables():
    fwd, inv = dft_table(LEN)
    f = fwd.astype(np.float32)
    i = inv.astype(np.float32)
    order = np.arange(KM).reshape(NH, NQ, BA).transpose(1, 0, 2).reshape(-1)
    ex = f[:, order].T
    ix = i[:, order].T
    eye_y = np.eye(GY, dtype=np.float32)
    eye_k = np.eye(BK, dtype=np.float32)
    kz = np.einsum("hqzgk,yw->hqyzgwk", f.reshape(NH, NQ, RZ, NGY, BK), eye_y)
    kz = kz.reshape(NH, NQ * GY * RZ, NGY * GY * BK)
    kzi = np.einsum("hqzgk,yw->hgykqwz", i.reshape(NH, NQ, RZ, NGY, BK), eye_y)
    kzi = kzi.reshape(NH, NGY * GY * BK, NQ * GY * RZ)
    ky = np.einsum("yb,kj->ykjb", f, eye_k).reshape(LEN * BK, BK * KM)
    kyi = np.einsum("yb,kj->kbyj", i, eye_k).reshape(BK * KM, LEN * BK)
    return tuple(np.ascontiguousarray(t).astype(ml_dtypes.bfloat16) for t in (ex, ix, kz, kzi, ky, kyi))


def iota(shape, axis):
    return lax.broadcasted_iota(jnp.int32, shape, axis)


def dot(a, b):
    return jnp.dot(a, b, preferred_element_type=F32)


def dot_nt(a, b):
    return lax.dot_general(a, b, (((1,), (1,)), ((), ())), preferred_element_type=F32)


def peer(place, off, ring):
    return (place // 2 + off // 2) % ring * 2 + (place + off) % 2


def swap_rows(first, second):
    low = iota(first.shape, 1) < BA
    return (
        jnp.where(low, first, pltpu.roll(second, BA, 1)),
        jnp.where(low, pltpu.roll(first, BA, 1), second),
    )


def swap_lanes(first, second):
    axis = first.ndim - 1
    low = iota(first.shape, axis) < 64
    return (
        jnp.where(low, first, pltpu.roll(second, 64, axis)),
        jnp.where(low, pltpu.roll(first, 64, axis), second),
    )


def gelu(x):
    inner = x * (math.sqrt(2.0 / math.pi) + (math.sqrt(2.0 / math.pi) * 0.044715) * (x * x))
    half = 0.5 * x
    return half + half * jnp.tanh(inner)


def kernel(
    forcing, lift_w, lift_b, point_w, spec_w, mixing, iterate, prev_it, prev_res,
    ex, ix, kz_all, kzi_all, ky_hbm, kyi_hbm,
    out, weights_out,
    v, pit, pres, step, forc, wts, lhs, xs, xr, xra, bs, br, pf, gs, gr, gsa, gra, hs, hg,
    kz, kzi, ky, kyi, qm, qt, qa, mo, osc, acc, ar1, ar2, ones,
    load_sem, in_sem, out_sem, loc_sem,
    xs_sem, xr_sem, xas_sem, xar_sem, bs_sem, br_sem, gs_sem, gr_sem, gas_sem, gar_sem, hs_sem, hr_sem,
    s1_sem, r1_sem, s2_sem, r2_sem,
):
    gy = lax.axis_index("gy")
    gz = lax.axis_index("gz")
    h = gz // NQ
    q = gz % NQ

    barrier = pltpu.get_barrier_semaphore()
    for off in range(1, 16):
        pl.semaphore_signal(barrier, inc=1, device_id=(gy, (gz + off) % 16), device_id_type=MESH)
    for dh, off in PEERS:
        if off:
            pl.semaphore_signal(
                barrier, inc=1, device_id=(peer(gy, off, NGY // 2), (h + dh) % NH * NQ + q),
                device_id_type=MESH)

    in_copies = [
        pltpu.make_async_copy(
            iterate.at[:, pl.ds(g * GY, GY)], v.at[:, pl.ds(g * GY, GY)], in_sem.at[g]
        )
        for g in range(GROUPS)
    ]
    loads = {
        name: pltpu.make_async_copy(src, dst, load_sem.at[n])
        for n, (name, src, dst) in enumerate([
            ("kz", kz_all.at[h], kz),
            ("pres", prev_res, pres),
            ("pit", prev_it, pit),
            ("ky", ky_hbm, ky),
            ("wts", spec_w, wts),
            ("kyi", kyi_hbm, kyi),
            ("kzi", kzi_all.at[h], kzi),
            ("forc", forcing, forc),
        ])
    }
    for copy in in_copies:
        copy.start()
    for copy in loads.values():
        copy.start()

    def to_q(src, dst, send_sem, recv_sem):
        def one(g, off):
            dest = peer(q, off, NQ // 2)
            return pltpu.make_async_remote_copy(
                src.at[g, dest], dst.at[g, q], send_sem.at[g, off], recv_sem.at[g, off],
                device_id=(gy, h * NQ + dest), device_id_type=MESH)
        return one

    send_x = to_q(xs, xr, xs_sem, xr_sem)
    send_a = to_q(xs, xra, xas_sem, xar_sem)
    send_b = to_q(bs, br, bs_sem, br_sem)

    def to_g(src, dst, send_sem, recv_sem):
        def one(p, dh, off):
            dest = peer(gy, off, NGY // 2)
            half = (h + dh) % NH
            return pltpu.make_async_remote_copy(
                src.at[p, half, dest], dst.at[p, h, gy],
                send_sem.at[p, dh, off], recv_sem.at[p, dh, off],
                device_id=(dest, half * NQ + q), device_id_type=MESH)
        return one

    send_g = to_g(gs, gr, gs_sem, gr_sem)
    send_ga = to_g(gsa, gra, gas_sem, gar_sem)

    def send_h(p, dh, off):
        dest = peer(gy, off, NGY // 2)
        return pltpu.make_async_remote_copy(
            hs.at[p, dest], hg.at[p, h, gy], hs_sem.at[p, dh, off], hr_sem.at[p, dh, off],
            device_id=(dest, (h + dh) % NH * NQ + q), device_id_type=MESH)

    def own_x(g):
        return pltpu.make_async_copy(xs.at[g, q], xr.at[g, q], loc_sem.at[g])

    def own_a(g):
        return pltpu.make_async_copy(xs.at[g, q], xra.at[g, q], loc_sem.at[4 + g])

    def own_b(g):
        return pltpu.make_async_copy(bs.at[g, q], br.at[g, q], loc_sem.at[8 + g])

    def own_g(p):
        return pltpu.make_async_copy(gs.at[p, h, gy], gr.at[p, h, gy], loc_sem.at[12 + p])

    def own_ga(p):
        return pltpu.make_async_copy(gsa.at[p, h, gy], gra.at[p, h, gy], loc_sem.at[14 + p])

    def own_h(p):
        return pltpu.make_async_copy(hs.at[p, gy], hg.at[p, h, gy], loc_sem.at[16 + p])

    def x_stage(g, field):
        for pair in range(C // 2):
            parts = []
            for j in range(2):
                rows = field(2 * pair + j, pl.ds(g * GY, GY)).reshape(GY * RZ, LEN)
                parts.append(dot_nt(ex[...], rows).reshape(NQ, NH * BA, GY * RZ))
            xs[g, :, pair * 16:(pair + 1) * 16, :] = jnp.concatenate(parts, axis=1).astype(BF)

    def field_x(c, ys):
        return v[c, ys]

    def field_a(c, ys):
        return (pit[c, ys].astype(F32) + mixing[c] * pres[c, ys].astype(F32)).astype(BF)

    def field_b(c, ys):
        return step[c, ys].astype(BF)

    def z_stage(g, src, dst):
        left = jnp.concatenate([src[g, s] for s in range(NQ)], axis=1)
        part = dot(left, kz[...]).reshape(C // 2, 2, 8, 512)
        halves = swap_rows(part[:, 0], part[:, 1])
        for half in range(NH):
            block = halves[half].reshape(HALF, 512)
            if g % 2 == 0:
                pf[half] = block
            else:
                for j in range(4):
                    cut = slice(j * 128, (j + 1) * 128)
                    even, odd = swap_lanes(pf[half, :, cut], block[:, cut])
                    dst[g // 2, half, 2 * j] = even.astype(BF)
                    dst[g // 2, half, 2 * j + 1] = odd.astype(BF)

    def y_stage(src):
        left = jnp.concatenate(
            [(src[p, 0, s].astype(F32) + src[p, 1, s].astype(F32)).astype(BF)
             for s in range(NGY) for p in range(2)], axis=1)
        return dot(left, ky[...])

    def mix_stage(sums):
        modes = sums.astype(BF).astype(F32).reshape(C // 2, 8, 512)
        for m in range(4):
            here = modes[:, :, m * 128:(m + 1) * 128]
            there = pltpu.roll(here, BA, 1)
            even, odd = swap_lanes(here, there)
            qm[2 * m * HALF:(2 * m + 1) * HALF, :] = even.reshape(HALF, 128)
            qm[(2 * m + 1) * HALF:(2 * m + 2) * HALF, :] = odd.reshape(HALF, 128)
        for a in range(BA):
            for t in range(C // 2):
                qt[a, t] = qm[pl.ds(t * 8 + a, BK, stride=HALF), :]

        def one(o, carry):
            for a in range(BA):
                total = jnp.zeros((BK, 128), F32)
                for t in range(C // 2):
                    total = total + wts[a, o, :, t * 128:(t + 1) * 128].astype(F32) * qt[a, t]
                row = pl.multiple_of((o * BA + a) * BK, BK)
                mo[pl.ds(row, BK), :] = total + pltpu.roll(total, 64, 1)
            return carry

        lax.fori_loop(0, C, one, 0)

    def yi_stage():
        low = iota((HALF, 128), 1) < 64
        left = jnp.concatenate(
            [jnp.where(low, mo[pl.ds(2 * m, HALF, stride=BK), :], mo[pl.ds(2 * m + 1, HALF, stride=BK), :])
             for m in range(4)], axis=1).astype(BF)
        for s in range(NGY):
            back = dot(left, kyi[:, s * 256:(s + 1) * 256]).astype(BF)
            hs[0, s] = back[:, :128]
            hs[1, s] = back[:, 128:]

    def zi_stage(p):
        cuts = {}
        for half in range(NH):
            for j in range(4):
                one = hg[p, half, 2 * j].astype(F32)
                two = hg[p, half, 2 * j + 1].astype(F32)
                cuts[half, j] = swap_lanes(one, two)
        for e in range(2):
            zero = jnp.concatenate([cuts[0, j][e] for j in range(4)], axis=1).reshape(C // 2, 8, 512)
            one = jnp.concatenate([cuts[1, j][e] for j in range(4)], axis=1).reshape(C // 2, 8, 512)
            even, odd = swap_rows(zero, one)
            left = jnp.concatenate([even, odd], axis=1).reshape(ROWS, 512).astype(BF)
            for s in range(0, NQ, 2):
                back = dot(left, kzi[:, s * 128:(s + 2) * 128]).astype(BF)
                bs[2 * p + e, s] = back[:, :128]
                bs[2 * p + e, s + 1] = back[:, 128:]

    def build_lhs():
        rows_o = iota((C * RZ, C), 0) // RZ
        pick = jnp.where(rows_o == iota((C * RZ, C), 1), 1.0, 0.0).astype(BF)
        col = iota((C, C * RZ), 1) // RZ
        spread = jnp.where(col == iota((C, C * RZ), 0), 1.0, 0.0).astype(BF)
        wide = dot(dot(pick, point_w[...]).astype(BF), spread)
        same = iota((C * RZ, C * RZ), 0) % RZ == iota((C * RZ, C * RZ), 1) % RZ
        wide = jnp.where(same, wide, 0.0)
        col3 = iota((3, 3 * RZ), 1) // RZ
        spread3 = jnp.where(col3 == iota((3, 3 * RZ), 0), 1.0, 0.0).astype(BF)
        lift = dot(dot_nt(pick, lift_w[...]).astype(BF), spread3)
        same3 = iota((C * RZ, 3 * RZ), 0) % RZ == iota((C * RZ, 3 * RZ), 1) % RZ
        lift = jnp.where(same3, lift, 0.0)
        bias = lift_b[...]
        hi = bias.astype(BF).astype(F32)
        mid = (bias - hi).astype(BF).astype(F32)
        lo = (bias - hi - mid).astype(BF).astype(F32)
        row = iota((16, C), 0)
        pieces = jnp.where(row == 0, hi, jnp.where(row == 1, mid, jnp.where(row == 2, lo, 0.0)))
        bias_cols = dot_nt(pick, pieces.astype(BF))
        full = jnp.concatenate([wide, lift, bias_cols], axis=1).astype(BF)
        for y in range(GY):
            lhs[y, :, 0:384] = full
        ones[...] = jnp.ones((16, LEN), BF)

    def turn_stage(g):
        for pair in range(C // 2):
            tile = br[g, :, pair * 16:(pair + 1) * 16, :].astype(F32)
            for j in range(2):
                block = tile[:, 8 * j:8 * j + 8].reshape(KM, GY * RZ)
                turned = jnp.transpose(block, (1, 0)).astype(BF).reshape(GY, RZ, KM)
                o = 2 * pair + j
                lhs[:, o * RZ:(o + 1) * RZ, 384:448] = turned

    def field_row(y):
        return v[:, y].reshape(C * RZ, LEN)

    def pre_activation(yl, y):
        right = jnp.concatenate(
            [field_row(y), forc[:, y].reshape(3 * RZ, LEN), ones[...], ix[...]], axis=0)
        osc[...] = dot(lhs[yl][:, :448], right)

    def final_first(g):
        turn_stage(g)

        def row(yl, carry):
            y = g * GY + yl
            pre_activation(yl, y)
            s_oo = jnp.zeros((RZ, LEN), F32)
            s_on = jnp.zeros((RZ, LEN), F32)
            s_nn = jnp.zeros((RZ, LEN), F32)
            for o in range(C):
                current = v[o, y].astype(F32)
                earlier = pres[o, y].astype(F32)
                newest = gelu(osc[o * RZ:(o + 1) * RZ, :]) - current
                step[o, y] = current + mixing[o] * newest
                s_oo += earlier * earlier
                s_on += earlier * newest
                s_nn += newest * newest
            acc[0] += s_oo
            acc[1] += s_on
            acc[2] += s_nn
            return carry

        lax.fori_loop(0, GY, row, 0)

    def final_second(g):
        turn_stage(g)

        def row(yl, carry):
            y = g * GY + yl
            pre_activation(yl, y)
            for o in range(C):
                current = v[o, y].astype(F32)
                pres[o, y] = (gelu(osc[o * RZ:(o + 1) * RZ, :]) - current).astype(BF)
            return carry

        lax.fori_loop(0, GY, row, 0)

    def combine(g, w_old, w_new):
        def one(c, carry):
            ys = pl.ds(g * GY, GY)
            old = pit[c, ys].astype(F32) + mixing[c] * pres[c, ys].astype(F32)
            v[c, ys] = (w_old * old + w_new * step[c, ys]).astype(BF)
            return carry

        lax.fori_loop(0, C, one, 0)

    def start_norms(kind):
        sends = []
        if kind == 0:
            rows = iota((8, 128), 0)
            mine = jnp.zeros((8, 128), F32)
            for n in range(3):
                total = jnp.sum(acc[n], axis=0, keepdims=True)
                mine = jnp.where(rows == n, total[:, :128] + total[:, 128:], mine)
            ar1[gz] = mine
            for off in range(1, 16):
                sends.append(pltpu.make_async_remote_copy(
                    ar1.at[gz], ar1.at[gz], s1_sem.at[off], r1_sem.at[off],
                    device_id=(gy, (gz + off) % 16), device_id_type=MESH))
        else:
            for off in range(1, 16):
                src = (gz - off + 16) % 16
                pltpu.make_async_remote_copy(
                    ar1.at[gz], ar1.at[src], s1_sem.at[off], r1_sem.at[off],
                    device_id=(gy, src), device_id_type=MESH).wait_recv()
            total = ar1[0]
            for s in range(1, 16):
                total = total + ar1[s]
            ar2[gy] = total
            for off in range(1, NGY):
                sends.append(pltpu.make_async_remote_copy(
                    ar2.at[gy], ar2.at[gy], s2_sem.at[off], r2_sem.at[off],
                    device_id=((gy + off) % NGY, gz), device_id_type=MESH))
        for copy in sends:
            copy.start()
        return sends

    def end_norms():
        for off in range(1, NGY):
            src = (gy - off + NGY) % NGY
            pltpu.make_async_remote_copy(
                ar2.at[gy], ar2.at[src], s2_sem.at[off], r2_sem.at[off],
                device_id=(src, gz), device_id_type=MESH).wait_recv()
        total = ar2[0]
        for s in range(1, NGY):
            total = total + ar2[s]
        sums = jnp.sum(total, axis=1, keepdims=True)
        norm_old, cross, norm_new = sums[0:1], sums[1:2], sums[2:3]
        ridge = REG * (norm_old + norm_new) + EPS
        denominator = norm_old + norm_new - 2.0 * cross + 2.0 * ridge
        w_old = (norm_new + ridge - cross) / denominator
        w_new = (norm_old + ridge - cross) / denominator
        weights_out[0] = w_old[0, 0]
        weights_out[1] = w_new[0, 0]
        return w_old, w_new

    def x_part(g):
        for off in range(1, NQ):
            send_x(g, off).start()
        own_x(g).start()

    def a_part(g):
        for off in range(1, NQ):
            send_x(g, off).wait_send()
        x_stage(g, field_a)
        for off in range(1, NQ):
            send_a(g, off).start()
        own_a(g).start()

    def b_part(g):
        for off in range(1, NQ):
            send_a(g, off).wait_send()
        x_stage(g, field_b)
        x_part(g)

    def z_part(g):
        own_x(g).wait()
        for off in range(1, NQ):
            send_x(g, off).wait_recv()
        z_stage(g, xr, gs)
        if g % 2 == 1:
            for dh, off in PEERS:
                send_g(g // 2, dh, off).start()
            own_g(g // 2).start()

    def za_part(g):
        own_a(g).wait()
        for off in range(1, NQ):
            send_a(g, off).wait_recv()
        z_stage(g, xra, gsa)
        if g % 2 == 1:
            for dh, off in PEERS:
                send_ga(g // 2, dh, off).start()
            own_ga(g // 2).start()

    def g_wait():
        for p in range(2):
            own_g(p).wait()
            for dh, off in PEERS:
                send_g(p, dh, off).wait_recv()

    def g_sent():
        for p in range(2):
            for dh, off in PEERS:
                send_g(p, dh, off).wait_send()

    def ga_wait():
        for p in range(2):
            own_ga(p).wait()
            for dh, off in PEERS:
                send_ga(p, dh, off).wait_recv()

    def h_part():
        yi_stage()
        for p in range(2):
            for dh, off in PEERS:
                send_h(p, dh, off).start()
            own_h(p).start()

    def zi_part(p):
        own_h(p).wait()
        for dh, off in PEERS:
            send_h(p, dh, off).wait_recv()
        zi_stage(p)
        for g in (2 * p, 2 * p + 1):
            for off in range(1, NQ):
                send_b(g, off).start()
            own_b(g).start()

    def b_wait(g):
        own_b(g).wait()
        for off in range(1, NQ):
            send_b(g, off).wait_recv()

    def inverse_sent():
        for p in range(2):
            for dh, off in PEERS:
                send_h(p, dh, off).wait_send()
        for g in range(GROUPS):
            for off in range(1, NQ):
                send_b(g, off).wait_send()

    for g in range(GROUPS):
        in_copies[g].wait()
        x_stage(g, field_x)
        if g == 0:
            pl.semaphore_wait(barrier, 29)
        x_part(g)
    acc[...] = jnp.zeros((3, RZ, LEN), F32)
    build_lhs()
    loads["kz"].wait()
    for g in range(GROUPS):
        z_part(g)
    loads["pres"].wait()
    loads["pit"].wait()
    a_part(0)
    a_part(1)
    for name in ("ky", "wts", "kyi", "kzi", "forc"):
        loads[name].wait()
    g_wait()
    mix_stage(y_stage(gr))
    h_part()
    a_part(2)
    a_part(3)
    zi_part(0)
    zi_part(1)
    g_sent()
    za_part(0)
    za_part(1)
    b_wait(0)
    final_first(0)
    b_part(0)
    za_part(2)
    za_part(3)
    for g in range(1, GROUPS):
        b_wait(g)
        final_first(g)
        b_part(g)
    sends = start_norms(0)
    inverse_sent()

    z_part(0)
    z_part(1)
    sends += start_norms(1)
    ga_wait()
    qa[...] = y_stage(gra)
    z_part(2)
    z_part(3)
    w_old, w_new = end_norms()
    g_wait()
    mix_stage(w_old * qa[...] + w_new * y_stage(gr))
    h_part()
    for g in range(GROUPS):
        combine(g, w_old.reshape(1, 1, 1), w_new.reshape(1, 1, 1))
    zi_part(0)
    zi_part(1)
    out_copies = []
    for g in range(GROUPS):
        b_wait(g)
        final_second(g)
        ys = pl.ds(g * GY, GY)
        out_copies.append(pltpu.make_async_copy(pres.at[:, ys], out.at[:, ys], out_sem.at[g]))
        out_copies[-1].start()
    for copy in sends:
        copy.wait_send()
    for g in range(GROUPS):
        for off in range(1, NQ):
            send_x(g, off).wait_send()
    g_sent()
    for p in range(2):
        for dh, off in PEERS:
            send_ga(p, dh, off).wait_send()
    inverse_sent()
    for copy in out_copies:
        copy.wait()


def shards(forcing, lift_weight, lift_bias, point_weight, spectral_weight, mixing, iterate, prev_iterate, prev_residual):
    ex, ix, kz, kzi, ky, kyi = (jnp.asarray(t) for t in tables())
    field = (C, RY, RZ, LEN)
    vmem = pl.BlockSpec(memory_space=pltpu.VMEM)
    smem = pl.BlockSpec(memory_space=pltpu.SMEM)
    hbm = pl.BlockSpec(memory_space=pl.ANY)
    dma = pltpu.SemaphoreType.DMA
    scratch = [
        pltpu.VMEM(field, BF),
        pltpu.VMEM(field, BF),
        pltpu.VMEM(field, BF),
        pltpu.VMEM(field, F32),
        pltpu.VMEM((3, RY, RZ, LEN), BF),
        pltpu.VMEM((BA, C, BK, C * KM), BF),
        pltpu.VMEM((GY, C * RZ, 512), BF),
        pltpu.VMEM((GROUPS, NQ, ROWS, 128), BF),
        pltpu.VMEM((GROUPS, NQ, ROWS, 128), BF),
        pltpu.VMEM((GROUPS, NQ, ROWS, 128), BF),
        pltpu.VMEM((GROUPS, NQ, ROWS, 128), BF),
        pltpu.VMEM((GROUPS, NQ, ROWS, 128), BF),
        pltpu.VMEM((NH, HALF, 512), F32),
        pltpu.VMEM((2, NH, NGY, HALF, 128), BF),
        pltpu.VMEM((2, NH, NGY, HALF, 128), BF),
        pltpu.VMEM((2, NH, NGY, HALF, 128), BF),
        pltpu.VMEM((2, NH, NGY, HALF, 128), BF),
        pltpu.VMEM((2, NGY, HALF, 128), BF),
        pltpu.VMEM((2, NH, NGY, HALF, 128), BF),
        pltpu.VMEM((1024, 512), BF),
        pltpu.VMEM((512, 1024), BF),
        pltpu.VMEM((2048, 512), BF),
        pltpu.VMEM((512, 2048), BF),
        pltpu.VMEM((BK * HALF, 128), F32),
        pltpu.VMEM((BA, C // 2, BK, 128), F32),
        pltpu.VMEM((HALF, 512), F32),
        pltpu.VMEM((BK * HALF, 128), F32),
        pltpu.VMEM((C * RZ, LEN), F32),
        pltpu.VMEM((3, RZ, LEN), F32),
        pltpu.VMEM((16, 8, 128), F32),
        pltpu.VMEM((NGY, 8, 128), F32),
        pltpu.VMEM((16, LEN), BF),
        dma((8,)), dma((GROUPS,)), dma((GROUPS,)), dma((18,)),
        dma((GROUPS, NQ)), dma((GROUPS, NQ)), dma((GROUPS, NQ)), dma((GROUPS, NQ)),
        dma((GROUPS, NQ)), dma((GROUPS, NQ)),
        dma((2, NH, NGY)), dma((2, NH, NGY)), dma((2, NH, NGY)), dma((2, NH, NGY)),
        dma((2, NH, NGY)), dma((2, NH, NGY)),
        dma((16,)), dma((16,)), dma((NGY,)), dma((NGY,)),
    ]
    result, weights = pl.pallas_call(
        kernel,
        out_shape=(
            jax.ShapeDtypeStruct(field, BF),
            jax.ShapeDtypeStruct((2,), F32),
        ),
        in_specs=[hbm, vmem, vmem, vmem, hbm, smem, hbm, hbm, hbm, vmem, vmem, hbm, hbm, hbm, hbm],
        out_specs=(hbm, smem),
        scratch_shapes=scratch,
        compiler_params=pltpu.CompilerParams(
            collective_id=0, has_side_effects=True, vmem_limit_bytes=60 * 1024 * 1024),
        cost_estimate=pl.CostEstimate(
            flops=10_000_000_000, bytes_accessed=40_000_000, transcendentals=5_000_000),
    )(forcing, lift_weight.T, lift_bias.reshape(1, C), point_weight,
      jnp.transpose(spectral_weight, (0, 2, 1, 3)), mixing,
      iterate, prev_iterate, prev_residual, ex, ix, kz, kzi, ky, kyi)
    return result, weights


def solution(mesh):
    in_specs = (
        P(None, "gy", "gz", None),
        P(),
        P(),
        P(),
        P("gz", "gy", None, None),
        P(),
        P(None, "gy", "gz", None),
        P(None, "gy", "gz", None),
        P(None, "gy", "gz", None),
    )
    out_specs = (P(None, "gy", "gz", None), P())
    return jax.shard_map(shards, mesh=mesh, in_specs=in_specs, out_specs=out_specs, check_vma=False)
```

time: 155 us -> 131 us (0.85)
  Pallas kernels: 143 us -> 124 us
  local copies, waits for them, and re-layouts: 10.9 us -> 5.83 us
    pallas_call x1, Pallas kernels: 143 us -> 124 us  [shards(): pl.pallas_call(kernel, out_shape=(jax.ShapeDtypeStruct(field, BF), jax.Sh...]
    unnamed x3 -> x4, local copies, waits for them, and re-layouts: 9.7 us -> 5.83 us
where the time goes in v2:
time: 131 us; the launch traced here: 130 us
  Pallas kernels  124 us (95%)
  local copies, waits for them, and re-layouts  5.83 us (4%)
    pallas_call x1, Pallas kernels, shards(): pl.pallas_call(kernel, out_shape=(jax.ShapeDtypeStruct(field, BF), jax.Sh...  124 us
    unnamed x4, local copies, waits for them, and re-layouts  5.83 us

profile of v2, /device:TPU:1, one launch (start us, length us, event | category | flops | bytes accessed | tf_op | source)
XLA Modules:
  0.0 130.4 jit_solution(9141224651185244832)
XLA Ops:
  0.6 123.9 %shard_map.158 = (bf16[20,32,16,256]{3,2,1,0:T(8,128)(2,1)}, f32[2]{0:T(128)}) custom-call(bf16[3,32,16,256]{3,2,1,0:T(8,128)(2,1)} %forcing.1, bf16[3,20]{1,0:T(4,128)(2,1)} %bitcast.4, f32[1,20]{1,0:T(1,128)} %bitcast.5, bf16[20,20]{1,0:T(8,128)(2,1)} %point_w.1, bf16[4,20,8,1280]{3,2,1,0:T(8,128)(2,1)} %bitcast.3, f32[20]{0:T(128)} %mixing.1, ...), custom_call_target="tpu_custom_call" | custom-call | flops 10000000000 | bytes 40000000 | tf_op jit(solution)/shard_map/pallas_call | solution.py:639
  124.5 0.0 copy-start
  124.5 5.3 %copy.19 = bf16[20,32,16,256]{3,2,1,0:T(8,128)(2,1)} copy(bf16[20,32,16,256]{3,2,1,0:T(8,128)(2,1)} %get-tuple-element.4) | data formatting | bytes 10485760
  129.9 0.0 copy-done
  129.9 0.5 copy.20
Async XLA Ops:
  124.5 5.3 %copy-start = (f32[2]{0:T(128)S(1)}, f32[2]{0:T(128)}, u32[]{:S(2)}) copy-start(f32[2]{0:T(128)} %get-tuple-element.5) | copy-start | bytes 28

commit v3 on v2

v3 whole, which is shorter than its diff:
```python
import functools
import math

import jax
import jax.numpy as jnp
import ml_dtypes
import numpy as np
from jax import lax
from jax.experimental import pallas as pl
from jax.experimental.pallas import tpu as pltpu
from jax.sharding import PartitionSpec as P

MESH = pl.DeviceIdType.MESH
BF = jnp.bfloat16
F32 = jnp.float32

MODES = 32
KM = 64
REG = 0.001
EPS = 1e-06

C = 20
LEN = 256
NGY = 8
NQ = 8
NH = 2
RY = 32
RZ = 16
GROUPS = 4
GY = 8
BA = 4
BK = 8
ROWS = C * NH * BA
HALF = C * BA


WIDE = 48


def ring_steps(off, ring):
    return min(off // 2, ring - off // 2)


PEERS = sorted(
    [(dh, off) for off in range(NGY) for dh in range(NH) if (dh, off) != (0, 0)],
    key=lambda t: -(ring_steps(t[1], NGY // 2) + (1 if t[1] % 2 else 2 * t[0])))
QPEERS = sorted(range(1, NQ), key=lambda t: -ring_steps(t, NQ // 2))


def dft_table(length):
    positions = np.arange(length)[:, None]
    waves = np.arange(2 * MODES)[None, :]
    number = np.where(waves < MODES, waves, waves - MODES + 1)
    angles = (positions * number % length).astype(np.float32) * np.float32(2.0 * math.pi / length)
    both = np.where(waves < MODES, np.cos(angles), np.sin(angles)).astype(np.float32)
    inverse = (both * np.float32(2.0 / length)).astype(ml_dtypes.bfloat16)
    return both.astype(ml_dtypes.bfloat16), inverse


@functools.lru_cache(maxsize=None)
def tables():
    fwd, inv = dft_table(LEN)
    f = fwd.astype(np.float32)
    i = inv.astype(np.float32)
    order = np.arange(KM).reshape(NH, NQ, BA).transpose(1, 0, 2).reshape(-1)
    ex = f[:, order].T
    ix = i[:, order].T
    eye_y = np.eye(GY, dtype=np.float32)
    eye_k = np.eye(BK, dtype=np.float32)
    kz = np.einsum("hqzgk,yw->hqyzgwk", f.reshape(NH, NQ, RZ, NGY, BK), eye_y)
    kz = kz.reshape(NH, NQ * GY * RZ, NGY * GY * BK)
    kzi = np.einsum("hqzgk,yw->hgykqwz", i.reshape(NH, NQ, RZ, NGY, BK), eye_y)
    kzi = kzi.reshape(NH, NGY * GY * BK, NQ * GY * RZ)
    ky = np.einsum("yb,kj->ykjb", f, eye_k).reshape(LEN * BK, BK * KM)
    kyi = np.einsum("yb,kj->kbyj", i, eye_k).reshape(BK * KM, LEN * BK)
    return tuple(np.ascontiguousarray(t).astype(ml_dtypes.bfloat16) for t in (ex, ix, kz, kzi, ky, kyi))


def iota(shape, axis):
    return lax.broadcasted_iota(jnp.int32, shape, axis)


def dot(a, b):
    return jnp.dot(a, b, preferred_element_type=F32)


def dot_nt(a, b):
    return lax.dot_general(a, b, (((1,), (1,)), ((), ())), preferred_element_type=F32)


def peer(place, off, ring):
    return (place // 2 + off // 2) % ring * 2 + (place + off) % 2


def swap_rows(first, second):
    low = iota(first.shape, 1) < BA
    return (
        jnp.where(low, first, pltpu.roll(second, BA, 1)),
        jnp.where(low, pltpu.roll(first, BA, 1), second),
    )


def swap_lanes(first, second):
    axis = first.ndim - 1
    low = iota(first.shape, axis) < 64
    return (
        jnp.where(low, first, pltpu.roll(second, 64, axis)),
        jnp.where(low, pltpu.roll(first, 64, axis), second),
    )


def gelu(x):
    inner = x * (math.sqrt(2.0 / math.pi) + (math.sqrt(2.0 / math.pi) * 0.044715) * (x * x))
    half = 0.5 * x
    return half + half * jnp.tanh(inner)


def kernel(
    forcing, lift_w, lift_b, point_w, spec_w, mixing, iterate, prev_it, prev_res,
    ex, ix, kz_all, kzi_all, ky_hbm, kyi_hbm,
    out, weights_out,
    v, pit, pres, step, forc, wts, lhs, xs, xr, xsa, xra, bs, br, gs, gr, gsa, gra, hs, hg,
    kz, kzi, ky, kyi, qm, qt, qa, mo, osc0, osc1, acc, ar1, ar2, ones,
    load_sem, in_sem, out_sem, loc_sem,
    xs_sem, xr_sem, xas_sem, xar_sem, bs_sem, br_sem, gs_sem, gr_sem, gas_sem, gar_sem, hs_sem, hr_sem,
    s1_sem, r1_sem, s2_sem, r2_sem,
):
    gy = lax.axis_index("gy")
    gz = lax.axis_index("gz")
    h = gz // NQ
    q = gz % NQ
    q_to = {off: peer(q, off, NQ // 2) for off in QPEERS}
    q_gz = {off: h * NQ + q_to[off] for off in QPEERS}
    y_to = {off: peer(gy, off, NGY // 2) for off in range(NGY)}
    h_to = [h, 1 - h]
    h_gz = [gz, (1 - h) * NQ + q]

    barrier = pltpu.get_barrier_semaphore()
    for dh, off in PEERS:
        pl.semaphore_signal(barrier, inc=1, device_id=(y_to[off], h_gz[dh]), device_id_type=MESH)
    for off in QPEERS:
        pl.semaphore_signal(barrier, inc=1, device_id=(gy, q_gz[off]), device_id_type=MESH)

    in_copies = [
        pltpu.make_async_copy(
            iterate.at[:, pl.ds(g * GY, GY)], v.at[:, pl.ds(g * GY, GY)], in_sem.at[g]
        )
        for g in range(GROUPS)
    ]
    loads = {
        name: pltpu.make_async_copy(src, dst, load_sem.at[n])
        for n, (name, src, dst) in enumerate([
            ("kz", kz_all.at[h], kz),
            ("pres", prev_res, pres),
            ("pit", prev_it, pit),
            ("ky", ky_hbm, ky),
            ("wts", spec_w, wts),
            ("kyi", kyi_hbm, kyi),
            ("kzi", kzi_all.at[h], kzi),
            ("forc", forcing, forc),
        ])
    }
    for copy in in_copies:
        copy.start()

    def to_q(src, dst, send_sem, recv_sem):
        def one(g, off):
            return pltpu.make_async_remote_copy(
                src.at[g, q_to[off]], dst.at[g, q], send_sem.at[g, off], recv_sem.at[g, off],
                device_id=(gy, q_gz[off]), device_id_type=MESH)
        return one

    send_x = to_q(xs, xr, xs_sem, xr_sem)
    send_a = to_q(xsa, xra, xas_sem, xar_sem)
    send_b = to_q(bs, br, bs_sem, br_sem)

    def to_g(src, dst, send_sem, recv_sem):
        def one(p, dh, off):
            return pltpu.make_async_remote_copy(
                src.at[p, h_to[dh], y_to[off]], dst.at[p, h, gy],
                send_sem.at[p, dh, off], recv_sem.at[p, dh, off],
                device_id=(y_to[off], h_gz[dh]), device_id_type=MESH)
        return one

    send_g = to_g(gs, gr, gs_sem, gr_sem)
    send_ga = to_g(gsa, gra, gas_sem, gar_sem)

    def send_h(p, dh, off):
        return pltpu.make_async_remote_copy(
            hs.at[p, y_to[off]], hg.at[p, h, gy], hs_sem.at[p, dh, off], hr_sem.at[p, dh, off],
            device_id=(y_to[off], h_gz[dh]), device_id_type=MESH)

    def own_x(g):
        return pltpu.make_async_copy(xs.at[g, q], xr.at[g, q], loc_sem.at[g])

    def own_a(g):
        return pltpu.make_async_copy(xsa.at[g, q], xra.at[g, q], loc_sem.at[4 + g])

    def own_b(g):
        return pltpu.make_async_copy(bs.at[g, q], br.at[g, q], loc_sem.at[8 + g])

    def own_g(p):
        return pltpu.make_async_copy(gs.at[p, h, gy], gr.at[p, h, gy], loc_sem.at[12 + p])

    def own_ga(p):
        return pltpu.make_async_copy(gsa.at[p, h, gy], gra.at[p, h, gy], loc_sem.at[16 + p])

    def own_h(p):
        return pltpu.make_async_copy(hs.at[p, gy], hg.at[p, h, gy], loc_sem.at[20 + p])

    def x_stage(g, field, dst):
        for pair in range(C // 2):
            parts = []
            for j in range(2):
                rows = field(2 * pair + j, pl.ds(g * GY, GY)).reshape(GY * RZ, LEN)
                parts.append(dot_nt(ex[...], rows).reshape(NQ, NH * BA, GY * RZ))
            dst[g, :, pair * 16:(pair + 1) * 16, :] = jnp.concatenate(parts, axis=1).astype(BF)

    def field_x(c, ys):
        return v[c, ys]

    def field_a(c, ys):
        return (pit[c, ys].astype(F32) + mixing[c] * pres[c, ys].astype(F32)).astype(BF)

    def field_b(c, ys):
        return step[c, ys].astype(BF)

    def z_stage(g, src, dst):
        left = jnp.concatenate([src[g, s] for s in range(NQ)], axis=1)
        part = dot(left, kz[...]).reshape(C // 2, 2, 8, 512)
        halves = swap_rows(part[:, 0], part[:, 1])
        for half in range(NH):
            block = halves[half].reshape(HALF, 512)
            for j in range(4):
                cut = block[:, j * 128:(j + 1) * 128]
                even, odd = swap_lanes(cut[:WIDE], cut[HALF - WIDE:])
                dst[g, half, 2 * j] = even.astype(BF)
                dst[g, half, 2 * j + 1] = odd.astype(BF)

    def unfold(first, second):
        top, bottom = swap_lanes(first, second)
        return jnp.concatenate([top, bottom[2 * WIDE - HALF:]], axis=0)

    def y_stage(src):
        parts = []
        for s in range(NGY):
            for p in range(2):
                pair = [src[g, 0, s].astype(F32) + src[g, 1, s].astype(F32) for g in (2 * p, 2 * p + 1)]
                parts.append(unfold(*pair).astype(BF))
        return dot(jnp.concatenate(parts, axis=1), ky[...])

    def mix_stage(sums):
        modes = sums.astype(BF).astype(F32).reshape(C // 2, 8, 512)
        for m in range(4):
            here = modes[:, :, m * 128:(m + 1) * 128]
            there = pltpu.roll(here, BA, 1)
            even, odd = swap_lanes(here, there)
            qm[2 * m * HALF:(2 * m + 1) * HALF, :] = even.reshape(HALF, 128)
            qm[(2 * m + 1) * HALF:(2 * m + 2) * HALF, :] = odd.reshape(HALF, 128)
        for a in range(BA):
            for t in range(C // 2):
                qt[a, t] = qm[pl.ds(t * 8 + a, BK, stride=HALF), :]

        def one(o, carry):
            for a in range(BA):
                total = jnp.zeros((BK, 128), F32)
                for t in range(C // 2):
                    total = total + wts[a, o, :, t * 128:(t + 1) * 128].astype(F32) * qt[a, t]
                row = pl.multiple_of((o * BA + a) * BK, BK)
                mo[pl.ds(row, BK), :] = total + pltpu.roll(total, 64, 1)
            return carry

        lax.fori_loop(0, C, one, 0, unroll=4)

    def yi_stage():
        low = iota((HALF, 128), 1) < 64
        left = jnp.concatenate(
            [jnp.where(low, mo[pl.ds(2 * m, HALF, stride=BK), :], mo[pl.ds(2 * m + 1, HALF, stride=BK), :])
             for m in range(4)], axis=1).astype(BF)
        for s in range(NGY):
            back = dot(left, kyi[:, s * 256:(s + 1) * 256])
            for p in range(2):
                cut = back[:, p * 128:(p + 1) * 128]
                even, odd = swap_lanes(cut[:WIDE], cut[HALF - WIDE:])
                hs[2 * p, s] = even.astype(BF)
                hs[2 * p + 1, s] = odd.astype(BF)

    def zi_stage(g):
        halves = [
            jnp.concatenate(
                [unfold(hg[g, half, 2 * j].astype(F32), hg[g, half, 2 * j + 1].astype(F32)) for j in range(4)],
                axis=1).reshape(C // 2, 8, 512)
            for half in range(NH)
        ]
        even, odd = swap_rows(*halves)
        left = jnp.concatenate([even, odd], axis=1).reshape(ROWS, 512).astype(BF)
        for s in range(0, NQ, 2):
            back = dot(left, kzi[:, s * 128:(s + 2) * 128]).astype(BF)
            bs[g, s] = back[:, :128]
            bs[g, s + 1] = back[:, 128:]

    def build_lhs():
        rows_o = iota((C * RZ, C), 0) // RZ
        pick = jnp.where(rows_o == iota((C * RZ, C), 1), 1.0, 0.0).astype(BF)
        col = iota((C, C * RZ), 1) // RZ
        spread = jnp.where(col == iota((C, C * RZ), 0), 1.0, 0.0).astype(BF)
        wide = dot(dot(pick, point_w[...]).astype(BF), spread)
        same = iota((C * RZ, C * RZ), 0) % RZ == iota((C * RZ, C * RZ), 1) % RZ
        wide = jnp.where(same, wide, 0.0)
        col3 = iota((3, 3 * RZ), 1) // RZ
        spread3 = jnp.where(col3 == iota((3, 3 * RZ), 0), 1.0, 0.0).astype(BF)
        lift = dot(dot_nt(pick, lift_w[...]).astype(BF), spread3)
        same3 = iota((C * RZ, 3 * RZ), 0) % RZ == iota((C * RZ, 3 * RZ), 1) % RZ
        lift = jnp.where(same3, lift, 0.0)
        bias = lift_b[...]
        hi = bias.astype(BF).astype(F32)
        mid = (bias - hi).astype(BF).astype(F32)
        lo = (bias - hi - mid).astype(BF).astype(F32)
        row = iota((16, C), 0)
        pieces = jnp.where(row == 0, hi, jnp.where(row == 1, mid, jnp.where(row == 2, lo, 0.0)))
        bias_cols = dot_nt(pick, pieces.astype(BF))
        full = jnp.concatenate([wide, lift, bias_cols], axis=1).astype(BF)
        for y in range(GY):
            lhs[y, :, 0:384] = full
        ones[...] = jnp.ones((16, LEN), BF)

    def turn_stage(g):
        for pair in range(C // 2):
            tile = br[g, :, pair * 16:(pair + 1) * 16, :].astype(F32)
            for j in range(2):
                block = tile[:, 8 * j:8 * j + 8].reshape(KM, GY * RZ)
                turned = jnp.transpose(block, (1, 0)).astype(BF).reshape(GY, RZ, KM)
                o = 2 * pair + j
                lhs[:, o * RZ:(o + 1) * RZ, 384:448] = turned

    def field_row(y):
        return v[:, y].reshape(C * RZ, LEN)

    def pre_activation(yl, y, dst):
        right = jnp.concatenate(
            [field_row(y), forc[:, y].reshape(3 * RZ, LEN), ones[...], ix[...]], axis=0)
        dst[...] = dot(lhs[yl][:, :448], right)

    def row_first(y, src):
        s_oo = jnp.zeros((RZ, LEN), F32)
        s_on = jnp.zeros((RZ, LEN), F32)
        s_nn = jnp.zeros((RZ, LEN), F32)
        for o in range(C):
            current = v[o, y].astype(F32)
            earlier = pres[o, y].astype(F32)
            newest = gelu(src[o * RZ:(o + 1) * RZ, :]) - current
            step[o, y] = current + mixing[o] * newest
            s_oo += earlier * earlier
            s_on += earlier * newest
            s_nn += newest * newest
        acc[0] += s_oo
        acc[1] += s_on
        acc[2] += s_nn

    def row_second(y, src):
        for o in range(C):
            current = v[o, y].astype(F32)
            pres[o, y] = (gelu(src[o * RZ:(o + 1) * RZ, :]) - current).astype(BF)

    def final(g, row):
        turn_stage(g)
        pre_activation(0, g * GY, osc0)

        def two_rows(i, carry):
            yl = 2 * i
            y = g * GY + yl
            pre_activation(yl + 1, y + 1, osc1)
            row(y, osc0)
            later = (yl + 2) % GY
            pre_activation(later, g * GY + later, osc0)
            row(y + 1, osc1)
            return carry

        lax.fori_loop(0, GY // 2, two_rows, 0)

    def combine(g, w_old, w_new):
        def one(c, carry):
            ys = pl.ds(g * GY, GY)
            old = pit[c, ys].astype(F32) + mixing[c] * pres[c, ys].astype(F32)
            v[c, ys] = (w_old * old + w_new * step[c, ys]).astype(BF)
            return carry

        lax.fori_loop(0, C, one, 0)

    def send_n1(off):
        return pltpu.make_async_remote_copy(
            ar1.at[q], ar1.at[q], s1_sem.at[off], r1_sem.at[off],
            device_id=(gy, q_gz[off]), device_id_type=MESH)

    def send_n2(dh, off):
        return pltpu.make_async_remote_copy(
            ar2.at[h, gy], ar2.at[h, gy], s2_sem.at[dh, off], r2_sem.at[dh, off],
            device_id=(y_to[off], h_gz[dh]), device_id_type=MESH)

    def start_norms():
        rows = iota((8, 128), 0)
        mine = jnp.zeros((8, 128), F32)
        for n in range(3):
            total = jnp.sum(acc[n], axis=0, keepdims=True)
            mine = jnp.where(rows == n, total[:, :128] + total[:, 128:], mine)
        ar1[q] = mine
        for off in QPEERS:
            send_n1(off).start()

    def next_norms():
        for off in QPEERS:
            send_n1(off).wait_recv()
        total = ar1[0]
        for s in range(1, NQ):
            total = total + ar1[s]
        ar2[h, gy] = total
        for dh, off in PEERS:
            send_n2(dh, off).start()

    def end_norms():
        for dh, off in PEERS:
            send_n2(dh, off).wait_recv()
        total = jnp.zeros((8, 128), F32)
        for half in range(NH):
            for s in range(NGY):
                total = total + ar2[half, s]
        sums = jnp.sum(total, axis=1, keepdims=True)
        norm_old, cross, norm_new = sums[0:1], sums[1:2], sums[2:3]
        ridge = REG * (norm_old + norm_new) + EPS
        denominator = norm_old + norm_new - 2.0 * cross + 2.0 * ridge
        w_old = (norm_new + ridge - cross) / denominator
        w_new = (norm_old + ridge - cross) / denominator
        weights_out[0] = w_old[0, 0]
        weights_out[1] = w_new[0, 0]
        return w_old, w_new

    def x_part(g):
        for off in QPEERS:
            send_x(g, off).start()
        own_x(g).start()

    def a_send(g):
        for off in QPEERS:
            send_a(g, off).start()
        own_a(g).start()

    def b_part(g):
        for off in QPEERS:
            send_x(g, off).wait_send()
        x_stage(g, field_b, xs)
        x_part(g)

    def z_part(g):
        own_x(g).wait()
        for off in QPEERS:
            send_x(g, off).wait_recv()
        z_stage(g, xr, gs)
        for dh, off in PEERS:
            send_g(g, dh, off).start()
        own_g(g).start()

    def za_part(g):
        own_a(g).wait()
        for off in QPEERS:
            send_a(g, off).wait_recv()
        z_stage(g, xra, gsa)
        for dh, off in PEERS:
            send_ga(g, dh, off).start()
        own_ga(g).start()

    def g_wait():
        for p in range(GROUPS):
            own_g(p).wait()
            for dh, off in PEERS:
                send_g(p, dh, off).wait_recv()

    def g_sent():
        for p in range(GROUPS):
            for dh, off in PEERS:
                send_g(p, dh, off).wait_send()

    def ga_wait():
        for p in range(GROUPS):
            own_ga(p).wait()
            for dh, off in PEERS:
                send_ga(p, dh, off).wait_recv()

    def h_part():
        yi_stage()
        h_send(0)
        h_send(1)

    def h_send(p):
        for dh, off in PEERS:
            send_h(p, dh, off).start()
        own_h(p).start()

    def zi_part(p):
        own_h(p).wait()
        for dh, off in PEERS:
            send_h(p, dh, off).wait_recv()
        zi_stage(p)
        for off in QPEERS:
            send_b(p, off).start()
        own_b(p).start()

    def b_wait(g):
        own_b(g).wait()
        for off in QPEERS:
            send_b(g, off).wait_recv()

    def inverse_sent():
        for p in range(GROUPS):
            for dh, off in PEERS:
                send_h(p, dh, off).wait_send()
        for g in range(GROUPS):
            for off in QPEERS:
                send_b(g, off).wait_send()

    for g in range(GROUPS):
        in_copies[g].wait()
        if g == 2:
            loads["kz"].start()
        x_stage(g, field_x, xs)
        if g == 0:
            pl.semaphore_wait(barrier, len(PEERS) + len(QPEERS))
        x_part(g)
    for name, copy in loads.items():
        if name != "kz":
            copy.start()
    acc[...] = jnp.zeros((3, RZ, LEN), F32)
    build_lhs()
    loads["kz"].wait()
    z_part(0)
    loads["pres"].wait()
    loads["pit"].wait()
    for g in range(1, GROUPS):
        x_stage(g - 1, field_a, xsa)
        z_part(g)
    for g in range(GROUPS - 1):
        a_send(g)
    x_stage(GROUPS - 1, field_a, xsa)
    a_send(GROUPS - 1)
    for name in ("ky", "wts", "kyi", "kzi", "forc"):
        loads[name].wait()
    g_wait()
    mix_stage(y_stage(gr))
    h_part()
    h_send(2)
    h_send(3)
    for g in range(GROUPS):
        zi_part(g)
    g_sent()
    za_part(0)
    za_part(1)
    b_wait(0)
    final(0, row_first)
    b_part(0)
    za_part(2)
    za_part(3)
    for g in range(1, GROUPS):
        b_wait(g)
        final(g, row_first)
        b_part(g)
    start_norms()
    inverse_sent()

    z_part(0)
    z_part(1)
    next_norms()
    ga_wait()
    qa[...] = y_stage(gra)
    z_part(2)
    z_part(3)
    w_old, w_new = end_norms()
    g_wait()
    mix_stage(w_old * qa[...] + w_new * y_stage(gr))
    h_part()
    parts = (w_old.reshape(1, 1, 1), w_new.reshape(1, 1, 1))
    combine(0, *parts)
    h_send(2)
    combine(1, *parts)
    h_send(3)
    for g in range(GROUPS):
        zi_part(g)
    combine(2, *parts)
    combine(3, *parts)
    out_copies = []
    for g in range(GROUPS):
        b_wait(g)
        final(g, row_second)
        ys = pl.ds(g * GY, GY)
        out_copies.append(pltpu.make_async_copy(pres.at[:, ys], out.at[:, ys], out_sem.at[g]))
        out_copies[-1].start()
    for off in QPEERS:
        send_n1(off).wait_send()
    for dh, off in PEERS:
        send_n2(dh, off).wait_send()
    for g in range(GROUPS):
        for off in QPEERS:
            send_x(g, off).wait_send()
            send_a(g, off).wait_send()
    g_sent()
    for p in range(GROUPS):
        for dh, off in PEERS:
            send_ga(p, dh, off).wait_send()
    inverse_sent()
    for copy in out_copies:
        copy.wait()


def shards(forcing, lift_weight, lift_bias, point_weight, spectral_weight, mixing, iterate, prev_iterate, prev_residual):
    ex, ix, kz, kzi, ky, kyi = (jnp.asarray(t) for t in tables())
    field = (C, RY, RZ, LEN)
    vmem = pl.BlockSpec(memory_space=pltpu.VMEM)
    smem = pl.BlockSpec(memory_space=pltpu.SMEM)
    hbm = pl.BlockSpec(memory_space=pl.ANY)
    dma = pltpu.SemaphoreType.DMA
    scratch = [
        pltpu.VMEM(field, BF),
        pltpu.VMEM(field, BF),
        pltpu.VMEM(field, BF),
        pltpu.VMEM(field, F32),
        pltpu.VMEM((3, RY, RZ, LEN), BF),
        pltpu.VMEM((BA, C, BK, C * KM), BF),
        pltpu.VMEM((GY, C * RZ, 512), BF),
        pltpu.VMEM((GROUPS, NQ, ROWS, 128), BF),
        pltpu.VMEM((GROUPS, NQ, ROWS, 128), BF),
        pltpu.VMEM((GROUPS, NQ, ROWS, 128), BF),
        pltpu.VMEM((GROUPS, NQ, ROWS, 128), BF),
        pltpu.VMEM((GROUPS, NQ, ROWS, 128), BF),
        pltpu.VMEM((GROUPS, NQ, ROWS, 128), BF),
        pltpu.VMEM((GROUPS, NH, NGY, WIDE, 128), BF),
        pltpu.VMEM((GROUPS, NH, NGY, WIDE, 128), BF),
        pltpu.VMEM((GROUPS, NH, NGY, WIDE, 128), BF),
        pltpu.VMEM((GROUPS, NH, NGY, WIDE, 128), BF),
        pltpu.VMEM((GROUPS, NGY, WIDE, 128), BF),
        pltpu.VMEM((GROUPS, NH, NGY, WIDE, 128), BF),
        pltpu.VMEM((1024, 512), BF),
        pltpu.VMEM((512, 1024), BF),
        pltpu.VMEM((2048, 512), BF),
        pltpu.VMEM((512, 2048), BF),
        pltpu.VMEM((BK * HALF, 128), F32),
        pltpu.VMEM((BA, C // 2, BK, 128), F32),
        pltpu.VMEM((HALF, 512), F32),
        pltpu.VMEM((BK * HALF, 128), F32),
        pltpu.VMEM((C * RZ, LEN), F32),
        pltpu.VMEM((C * RZ, LEN), F32),
        pltpu.VMEM((3, RZ, LEN), F32),
        pltpu.VMEM((NQ, 8, 128), F32),
        pltpu.VMEM((NH, NGY, 8, 128), F32),
        pltpu.VMEM((16, LEN), BF),
        dma((8,)), dma((GROUPS,)), dma((GROUPS,)), dma((24,)),
        dma((GROUPS, NQ)), dma((GROUPS, NQ)), dma((GROUPS, NQ)), dma((GROUPS, NQ)),
        dma((GROUPS, NQ)), dma((GROUPS, NQ)),
        dma((GROUPS, NH, NGY)), dma((GROUPS, NH, NGY)), dma((GROUPS, NH, NGY)), dma((GROUPS, NH, NGY)),
        dma((GROUPS, NH, NGY)), dma((GROUPS, NH, NGY)),
        dma((NQ,)), dma((NQ,)), dma((NH, NGY)), dma((NH, NGY)),
    ]
    result, weights = pl.pallas_call(
        kernel,
        out_shape=(
            jax.ShapeDtypeStruct(field, BF),
            jax.ShapeDtypeStruct((2,), F32),
        ),
        in_specs=[hbm, vmem, vmem, vmem, hbm, smem, hbm, hbm, hbm, vmem, vmem, hbm, hbm, hbm, hbm],
        out_specs=(hbm, smem),
        scratch_shapes=scratch,
        compiler_params=pltpu.CompilerParams(
            collective_id=0, has_side_effects=True, vmem_limit_bytes=60 * 1024 * 1024),
        cost_estimate=pl.CostEstimate(
            flops=10_000_000_000, bytes_accessed=40_000_000, transcendentals=5_000_000),
    )(forcing, lift_weight.T, lift_bias.reshape(1, C), point_weight,
      jnp.transpose(spectral_weight, (0, 2, 1, 3)), mixing,
      iterate, prev_iterate, prev_residual, ex, ix, kz, kzi, ky, kyi)
    return result, weights


def solution(mesh):
    in_specs = (
        P(None, "gy", "gz", None),
        P(),
        P(),
        P(),
        P("gz", "gy", None, None),
        P(),
        P(None, "gy", "gz", None),
        P(None, "gy", "gz", None),
        P(None, "gy", "gz", None),
    )
    out_specs = (P(None, "gy", "gz", None), P())
    return jax.shard_map(shards, mesh=mesh, in_specs=in_specs, out_specs=out_specs, check_vma=False)
```

time: 131 us -> 120 us (0.916)
  Pallas kernels: 124 us -> 113 us
    pallas_call x1, Pallas kernels: 124 us -> 113 us  [shards(): pl.pallas_call(kernel, out_shape=(jax.ShapeDtypeStruct(field, BF), jax.Sh...]
where the time goes in v3:
time: 120 us
  Pallas kernels  113 us (94%)
  local copies, waits for them, and re-layouts  5.83 us (5%)
    pallas_call x1, Pallas kernels, shards(): pl.pallas_call(kernel, out_shape=(jax.ShapeDtypeStruct(field, BF), jax.Sh...  113 us
    unnamed x4, local copies, waits for them, and re-layouts  5.83 us

profile of v3, /device:TPU:1, one launch (start us, length us, event | category | flops | bytes accessed | tf_op | source)
XLA Modules:
  0.0 119.6 jit_solution(3988361166629012084)
XLA Ops:
  0.6 113.1 %shard_map.158 = (bf16[20,32,16,256]{3,2,1,0:T(8,128)(2,1)}, f32[2]{0:T(128)}) custom-call(bf16[3,32,16,256]{3,2,1,0:T(8,128)(2,1)} %forcing.1, bf16[3,20]{1,0:T(4,128)(2,1)} %bitcast.4, f32[1,20]{1,0:T(1,128)} %bitcast.5, bf16[20,20]{1,0:T(8,128)(2,1)} %point_w.1, bf16[4,20,8,1280]{3,2,1,0:T(8,128)(2,1)} %bitcast.3, f32[20]{0:T(128)} %mixing.1, ...), custom_call_target="tpu_custom_call" | custom-call | flops 10000000000 | bytes 40000000 | tf_op jit(solution)/shard_map/pallas_call | solution.py:660
  113.8 0.0 copy-start
  113.8 5.3 %copy.19 = bf16[20,32,16,256]{3,2,1,0:T(8,128)(2,1)} copy(bf16[20,32,16,256]{3,2,1,0:T(8,128)(2,1)} %get-tuple-element.4) | data formatting | bytes 10485760
  119.1 0.0 copy-done
  119.1 0.5 copy.20
Async XLA Ops:
  113.8 5.3 %copy-start = (f32[2]{0:T(128)S(1)}, f32[2]{0:T(128)}, u32[]{:S(2)}) copy-start(f32[2]{0:T(128)} %get-tuple-element.5) | copy-start | bytes 28

commit v4 on v3

--- a/solution.py
+++ b/solution.py
@@ -403,27 +403,27 @@
         for n in range(3):
             total = jnp.sum(acc[n], axis=0, keepdims=True)
             mine = jnp.where(rows == n, total[:, :128] + total[:, 128:], mine)
-        ar1[q] = mine
-        for off in QPEERS:
-            send_n1(off).start()
-
-    def next_norms():
-        for off in QPEERS:
-            send_n1(off).wait_recv()
-        total = ar1[0]
-        for s in range(1, NQ):
-            total = total + ar1[s]
-        ar2[h, gy] = total
+        ar2[h, gy] = mine
         for dh, off in PEERS:
             send_n2(dh, off).start()
 
-    def end_norms():
+    def next_norms():
         for dh, off in PEERS:
             send_n2(dh, off).wait_recv()
         total = jnp.zeros((8, 128), F32)
         for half in range(NH):
             for s in range(NGY):
                 total = total + ar2[half, s]
+        ar1[q] = total
+        for off in QPEERS:
+            send_n1(off).start()
+
+    def end_norms():
+        for off in QPEERS:
+            send_n1(off).wait_recv()
+        total = ar1[0]
+        for s in range(1, NQ):
+            total = total + ar1[s]
         sums = jnp.sum(total, axis=1, keepdims=True)
         norm_old, cross, norm_new = sums[0:1], sums[1:2], sums[2:3]
         ridge = REG * (norm_old + norm_new) + EPS
@@ -561,8 +561,9 @@
     for g in range(1, GROUPS):
         b_wait(g)
         final(g, row_first)
+        if g == GROUPS - 1:
+            start_norms()
         b_part(g)
-    start_norms()
     inverse_sent()
 
     z_part(0)

time: 120 us -> 117 us (0.975)
  Pallas kernels: 113 us -> 110 us
    pallas_call x1, Pallas kernels: 113 us -> 110 us  [shards(): pl.pallas_call(kernel, out_shape=(jax.ShapeDtypeStruct(field, BF), jax.Sh...]
where the time goes in v4:
time: 117 us
  Pallas kernels  110 us (94%)
  local copies, waits for them, and re-layouts  5.83 us (5%)
    pallas_call x1, Pallas kernels, shards(): pl.pallas_call(kernel, out_shape=(jax.ShapeDtypeStruct(field, BF), jax.Sh...  110 us
    unnamed x4, local copies, waits for them, and re-layouts  5.83 us

profile of v4, /device:TPU:1, one launch (start us, length us, event | category | flops | bytes accessed | tf_op | source)
XLA Modules:
  0.0 116.9 jit_solution(10204396617977744497)
XLA Ops:
  0.6 110.5 %shard_map.158 = (bf16[20,32,16,256]{3,2,1,0:T(8,128)(2,1)}, f32[2]{0:T(128)}) custom-call(bf16[3,32,16,256]{3,2,1,0:T(8,128)(2,1)} %forcing.1, bf16[3,20]{1,0:T(4,128)(2,1)} %bitcast.4, f32[1,20]{1,0:T(1,128)} %bitcast.5, bf16[20,20]{1,0:T(8,128)(2,1)} %point_w.1, bf16[4,20,8,1280]{3,2,1,0:T(8,128)(2,1)} %bitcast.3, f32[20]{0:T(128)} %mixing.1, ...), custom_call_target="tpu_custom_call" | custom-call | flops 10000000000 | bytes 40000000 | tf_op jit(solution)/shard_map/pallas_call | solution.py:661
  111.1 0.0 copy-start
  111.1 5.3 %copy.19 = bf16[20,32,16,256]{3,2,1,0:T(8,128)(2,1)} copy(bf16[20,32,16,256]{3,2,1,0:T(8,128)(2,1)} %get-tuple-element.4) | data formatting | bytes 10485760
  116.4 0.0 copy-done
  116.4 0.5 copy.20
Async XLA Ops:
  111.1 5.3 %copy-start = (f32[2]{0:T(128)S(1)}, f32[2]{0:T(128)}, u32[]{:S(2)}) copy-start(f32[2]{0:T(128)} %get-tuple-element.5) | copy-start | bytes 28

commit v5 on v4

--- a/solution.py
+++ b/solution.py
@@ -548,16 +548,16 @@
     h_part()
     h_send(2)
     h_send(3)
+    za_part(0)
+    za_part(1)
     for g in range(GROUPS):
         zi_part(g)
     g_sent()
-    za_part(0)
-    za_part(1)
+    za_part(2)
+    za_part(3)
     b_wait(0)
     final(0, row_first)
     b_part(0)
-    za_part(2)
-    za_part(3)
     for g in range(1, GROUPS):
         b_wait(g)
         final(g, row_first)

time: 117 us -> 117 us (level)
  no operation moved by 1% of the time
where the time goes in v5:
time: 117 us
  Pallas kernels  110 us (94%)
  local copies, waits for them, and re-layouts  5.83 us (5%)
    pallas_call x1, Pallas kernels, shards(): pl.pallas_call(kernel, out_shape=(jax.ShapeDtypeStruct(field, BF), jax.Sh...  110 us
    unnamed x4, local copies, waits for them, and re-layouts  5.83 us

profile of v5, /device:TPU:1, one launch (start us, length us, event | category | flops | bytes accessed | tf_op | source)
XLA Modules:
  0.0 116.9 jit_solution(9425584760057628164)
XLA Ops:
  0.6 110.5 %shard_map.158 = (bf16[20,32,16,256]{3,2,1,0:T(8,128)(2,1)}, f32[2]{0:T(128)}) custom-call(bf16[3,32,16,256]{3,2,1,0:T(8,128)(2,1)} %forcing.1, bf16[3,20]{1,0:T(4,128)(2,1)} %bitcast.4, f32[1,20]{1,0:T(1,128)} %bitcast.5, bf16[20,20]{1,0:T(8,128)(2,1)} %point_w.1, bf16[4,20,8,1280]{3,2,1,0:T(8,128)(2,1)} %bitcast.3, f32[20]{0:T(128)} %mixing.1, ...), custom_call_target="tpu_custom_call" | custom-call | flops 10000000000 | bytes 40000000 | tf_op jit(solution)/shard_map/pallas_call | solution.py:661
  111.1 0.0 copy-start
  111.1 5.3 %copy.19 = bf16[20,32,16,256]{3,2,1,0:T(8,128)(2,1)} copy(bf16[20,32,16,256]{3,2,1,0:T(8,128)(2,1)} %get-tuple-element.4) | data formatting | bytes 10485760
  116.4 0.0 copy-done
  116.4 0.5 copy.20
Async XLA Ops:
  111.1 5.3 %copy-start = (f32[2]{0:T(128)S(1)}, f32[2]{0:T(128)}, u32[]{:S(2)}) copy-start(f32[2]{0:T(128)} %get-tuple-element.5) | copy-start | bytes 28
